TPU v7x, 512 devices: a whole 4x8x8 slice. The times are simulated.
512 devices in a mesh: ky: 64 (over y_lo, z, core), gz: 8 (over y_hi, x).
Axes of the slice: x: 4, y: 8 (y_hi: 2, y_lo: 4; y = y_hi * 4 + y_lo), z: 8, core: 2. Of those that a mesh axis runs over, the one named last changes fastest.
Arguments:
- amplitudes: float32 [2, 512, 1024], P(None, 'ky'), may hold values from -0.046875 to 0.046875
- complementary: float32 [128, 8, 3, 256], P('ky', None, None, 'gz'), may hold values from -6 to 6
Outputs:
- incident: float32 [128, 8, 3, 256], P('ky', None, None, 'gz')
- predicted: float32 [128, 8, 3, 256], P('ky', None, None, 'gz')
All inputs are finite; a program needn't handle non-finite values.
Results may differ from a plain program's by a relative error of at most 0.000088.
Values sent between devices are 32-bit elements; how exact they have to be, the bound alone decides.
No kernel may reach another device: no remote copies, remote signals or barrier semaphores. Data moves between devices by JAX's collectives and lax.ppermute only.
A program may use at most 64 MiB of HBM per device.

v0:
```python
import jax
import jax.numpy as jnp
from jax import lax
from jax.sharding import PartitionSpec as P

band_factor = 16.0
cell_height = 0.125
time_step = 0.05
viscosity = 0.02


def extended(x, sides, width):
    for axis, dim in sides:
        size, length = (lax.axis_size(axis), x.shape[dim])
        up = [(i, (i + 1) % size) for i in range(size - 1)]
        down = [(j, i) for i, j in up]
        last = lax.slice_in_dim(x, length - width, length, axis=dim)
        initial = lax.slice_in_dim(x, 0, width, axis=dim)
        before = lax.ppermute(last, axis, up)
        after = lax.ppermute(initial, axis, down)
        x = jnp.concatenate([before, x, after], axis=dim)
    return x


def wave_numbers_y(wave_rows, wave_count):
    return 2.0 * jnp.pi * (wave_rows - wave_count / 2.0) / (band_factor * wave_count)


def x_section(real_part, imag_part, wave_rows, wave_count, x_points, depths):
    kx_count = real_part.shape[1]
    along_x = 2.0 * jnp.pi * jnp.arange(kx_count, dtype=jnp.float32) / (band_factor * kx_count)
    along_y = wave_numbers_y(wave_rows, wave_count)
    magnitude = jnp.sqrt(along_x[None, :] ** 2 + along_y[:, None] ** 2)
    decay_factor = jnp.exp(magnitude[None] * depths[:, None, None])
    scaled_re = decay_factor * real_part[None]
    scaled_im = decay_factor * imag_part[None]
    factor_x = along_x[None, None, :]
    factor_y = along_y[None, :, None]
    factor_k = magnitude[None]
    parts_re = jnp.stack(
        [-factor_x * scaled_im, -factor_y * scaled_im, factor_k * scaled_re], axis=1
    )
    parts_im = jnp.stack([factor_x * scaled_re, factor_y * scaled_re, factor_k * scaled_im], axis=1)
    stacked = jnp.stack([parts_re, parts_im], axis=2)
    level_count = stacked.shape[0]
    wave_local = stacked.shape[3]
    flat_modes = stacked.reshape(-1, kx_count)
    phase_x = along_x[:, None] * x_points[None, :]
    table_x = jnp.concatenate([jnp.cos(phase_x), jnp.sin(phase_x)], axis=1)
    product = jnp.dot(
        flat_modes, table_x, precision=lax.Precision.HIGHEST, preferred_element_type=jnp.float32
    )
    product = product.reshape(level_count, 3, 2, wave_local, 2, x_points.shape[0])
    real_x = product[:, :, 0, :, 0] - product[:, :, 1, :, 1]
    imag_x = product[:, :, 0, :, 1] + product[:, :, 1, :, 0]
    return jnp.stack([real_x, -imag_x], axis=2)


def y_section(transformed, wave_rows, wave_count, y_points):
    level_count = transformed.shape[0]
    row_count = transformed.shape[3]
    combined = transformed.reshape(level_count, 3, 2 * row_count, transformed.shape[4])
    along_y = wave_numbers_y(wave_rows, wave_count)
    phase_y = along_y[:, None] * y_points[None, :]
    table_y = jnp.concatenate([jnp.cos(phase_y), jnp.sin(phase_y)], axis=0)
    return jnp.einsum("lcnx,ny->xlcy", combined, table_y, precision=lax.Precision.HIGHEST)


def incident_block(real_part, imag_part, wave_rows, wave_count, x_points, depths, y_points):
    transformed = x_section(real_part, imag_part, wave_rows, wave_count, x_points, depths)
    return y_section(transformed, wave_rows, wave_count, y_points)


def trimmed(array_in, axis_cut, first_index, index_count):
    result = array_in
    for other_axis in (0, 1, 3):
        if other_axis == axis_cut:
            result = lax.slice_in_dim(
                result, first_index, first_index + index_count, axis=other_axis
            )
        else:
            result = lax.slice_in_dim(result, 1, result.shape[other_axis] - 1, axis=other_axis)
    return result


def predict(padded):
    expanded = jnp.pad(padded, ((0, 0), (1, 1), (0, 0), (0, 0)))
    centre_uc = trimmed(expanded, 1, 1, expanded.shape[1] - 2)[:, :, 3:]
    tendency = jnp.zeros_like(centre_uc)
    for spatial, normal, spacing in ((0, 0, 1.0), (3, 1, 1.0), (1, 2, cell_height)):
        inner_count = expanded.shape[spatial] - 2
        lower_cells = trimmed(expanded, spatial, 0, inner_count + 1)
        upper_cells = trimmed(expanded, spatial, 1, inner_count + 1)
        face_values = 0.5 * (lower_cells + upper_cells)
        face_inc = face_values[:, :, :3]
        face_comp = face_values[:, :, 3:]
        normal_total = face_inc[:, :, normal] + face_comp[:, :, normal]
        face_flux = (
            normal_total[:, :, None] * face_comp + face_comp[:, :, normal][:, :, None] * face_inc
        )
        divergence = (
            lax.slice_in_dim(face_flux, 1, inner_count + 1, axis=spatial)
            - lax.slice_in_dim(face_flux, 0, inner_count, axis=spatial)
        ) / spacing
        neighbours = (
            trimmed(expanded, spatial, 0, inner_count)[:, :, 3:]
            + trimmed(expanded, spatial, 2, inner_count)[:, :, 3:]
        )
        tendency = (
            tendency - divergence + viscosity * (neighbours - 2.0 * centre_uc) / (spacing * spacing)
        )
    return centre_uc + time_step * tendency


def on_device(amplitudes, complementary):
    x_tile = complementary.shape[0]
    depth_count = complementary.shape[1]
    y_tile = complementary.shape[3]
    ky_groups = lax.axis_size("ky")
    gz_groups = lax.axis_size("gz")
    level_count = depth_count // gz_groups
    wave_local = amplitudes.shape[1]
    wave_count = wave_local * ky_groups
    zone_y = y_tile * gz_groups
    level_first = lax.axis_index("gz") * level_count
    depths = (
        -((level_first + jnp.arange(level_count, dtype=jnp.int32)).astype(jnp.float32) + 0.5)
        * cell_height
    )
    y_points = jnp.arange(zone_y, dtype=jnp.float32) + 0.5
    x_first = lax.axis_index("ky") * x_tile
    x_points = (x_first + jnp.arange(x_tile, dtype=jnp.int32)).astype(jnp.float32) + 0.5
    shard_piece = lax.all_gather(amplitudes, "ky", axis=1, tiled=True)
    wave_rows = jnp.arange(shard_piece.shape[1], dtype=jnp.int32).astype(jnp.float32)
    partial_field = incident_block(
        shard_piece[0], shard_piece[1], wave_rows, wave_count, x_points, depths, y_points
    )
    incident = lax.all_to_all(partial_field, "gz", split_axis=3, concat_axis=1, tiled=True)
    stacked = jnp.concatenate([incident, complementary], axis=2)
    padded = extended(stacked, (("ky", 0), ("gz", 3)), 1)
    return (incident, predict(padded))


def solution(mesh):
    placed = (P(None, "ky", None), P("ky", None, None, "gz"))
    return jax.shard_map(
        on_device,
        mesh=mesh,
        in_specs=placed,
        out_specs=(P("ky", None, None, "gz"), P("ky", None, None, "gz")),
        check_vma=False,
    )
```

profile of v0, /device:TPU:14, one launch (start us, length us, event | category | flops | bytes accessed | tf_op | source)
XLA Modules:
  0.0 205.7 jit_solution(8816628980728699761)
XLA Ops:
  7.2 0.7 all-gather.2.cloned.1.call-update
  7.9 0.2 multiply_cosine_fusion.1
  8.3 1.9 multiply_cosine_fusion
  10.1 123.8 %all-gather.2.cloned.1.call-done = f32[2,512,1024]{2,1,0:T(8,128)} async-done(((f32[2,8,1024]{2,1,0:T(8,128)}), f32[2,512,1024]{2,1,0:T(8,128)}) %all-gather.2.cloned.1.call-update) | async-done | bytes 4194320 | tf_op jit(solution)/shard_map/all_gather | solution.py:133
  134.0 3.2 %multiply_bitcast_fusion.5 = (f32[1,1,512,1024]{3,2,1,0:T(8,128)S(1)}, f32[1,1,512,1024]{3,2,1,0:T(8,128)S(1)}, f32[1,1,512,1024]{3,2,1,0:T(8,128)S(1)}, f32[1,1...) fusion(f32[1024]{0:T(1024)S(1)} %fusion.36, ...), kind=kLoop, calls=%fused_computation.13 | loop fusion | flops 5242880 | bytes 16795652 | tf_op jit(solution)/shard_map/stack | solution.py:40
  137.2 2.3 %maximum_bitcast_fusion.2 = (f32[1,3,1,512,1024]{4,3,2,1,0:T(8,128)S(1)}, f32[1,3,1,512,1024]{4,3,2,1,0:T(8,128)S(1)}) fusion(f32[1,1,512,1024]{3,2,1,0:T(8,128)S(1)} %get-tuple-element.11, f32[1,1,512,1024]{3,2,1,0:T(8,128)S(1)} %get-tuple-element.9, f32[1,1,512,1024]{3,2,1,0:T(8,128)S(1)} %get-tuple-element.6, ...), kind=kLoop, calls=%fused_computation.4 | loop fusion | flops 6291456 | bytes 25165824 | tf_op jit(solution)/shard_map/stack | solution.py:44
  139.5 10.6 %fusion.3 = f32[1,3,2,512,2,2]{3,5,4,2,1,0:T(2,128)S(1)} fusion(f32[1,3,1,512,1024]{4,3,2,1,0:T(8,128)S(1)} %get-tuple-element.32, f32[1,3,1,512,1024]{4,3,2,1,0:T(8,128)S(1)} %get-tuple-element.31, f32[2,2,1024,1,1]{2,1,0,3,4:T(2,128)S(1)} %reshape.233), kind=kOutput, calls=%fused_computation.16 | convolution fusion | flops 154140672 | bytes 12648448 | tf_op jit(solution)/shard_map/dot_general | solution.py:50
  150.2 0.6 convolution_bitcast_fusion
  150.9 0.2 copy.23
  151.0 0.4 reshape.237
  151.4 17.5 %all_to_all.18 = f32[8,1,192]{2,1,0:T(1,128)S(1)} all-to-all(f32[8,1,192]{2,1,0:T(1,128)S(1)} %reshape.237), channel_id=1, replica_groups=mesh['ky'=64,'gz'=8] {'gz'}, dimensions={0} | all-to-all | bytes 12288 | tf_op jit(solution)/shard_map/all_to_all | solution.py:138
  169.0 0.5 broadcast.193
  169.5 0.7 reduce
  170.1 0.4 reshape.238
  170.7 1.9 collective-permute-start
  172.7 5.8 %collective-permute-start.1 = (f32[1,8,6,32]{3,1,0,2:T(8,128)S(1)}, f32[1,8,6,32]{3,1,0,2:T(8,128)S(1)}, u32[]{:S(2)}, u32[]{:S(2)}) collective-permute-start(f32[1,8,6,32]{3,1,0,2:T(8,128)S(1)} %get-tuple-element.26), channel_id=1, source_target_pairs={{8,0},{16,8},{24,16},{32,24},{40,32},{48,40},{56,48},{64,56},{72,6... | collective-permute-start | bytes 18440 | tf_op jit(solution)/shard_map/ppermute | solution.py:20
  178.4 0.8 copy.34
  179.2 0.7 collective-permute-done.1
  180.1 4.0 %collective-permute-start.2 = (f32[4,8,6,1]{3,1,0,2:T(8,128)S(1)}, f32[4,8,6,1]{3,1,0,2:T(8,128)S(1)}, u32[]{:S(2)}, u32[]{:S(2)}) collective-permute-start(f32[4,8,6,1]{3,1,0,2:T(8,128)S(1)} %get-tuple-element.16), channel_id=1, source_target_pairs={{0,1},{1,2},{2,3},{3,4},{4,5},{5,6},{6,7},{8,9},{9,10},{10,11},{11... | collective-permute-start | bytes 2312 | tf_op jit(solution)/shard_map/ppermute | solution.py:19
  184.1 1.9 collective-permute-start.3
  186.0 1.3 collective-permute-done.2
  187.3 10.4 %collective-permute-done.3 = f32[4,8,6,1]{3,1,0,2:T(8,128)S(1)} collective-permute-done((f32[4,8,6,1]{3,1,0,2:T(8,128)S(1)}, f32[4,8,6,1]{3,1,0,2:T(8,128)S(1)}, u32[]{:S(2)}, u32[]{:S(2)}) %collective-permute-start.3) | collective-permute-done | bytes 800 | tf_op jit(solution)/shard_map/ppermute | solution.py:20
  197.8 0.2 select_maximum_fusion
  198.3 0.6 copy.29
  (35 shorter events, 0.9 us)
Async XLA Ops:
  7.2 126.8 %all-gather.2.cloned.1.call-start = ((), (), s32[]{:S(2)}) async-start(), calls=%async_computation.1 | async-start | bytes 4259840 | tf_op jit(solution)/shard_map/all_gather | solution.py:133
  150.1 20.6 %copy-start = (f32[2,8,3,32]{3,1,2,0:T(8,128)S(1)}, f32[2,8,3,32]{3,1,2,0:T(8,128)}, u32[]{:S(2)}) copy-start(f32[2,8,3,32]{3,1,2,0:T(8,128)} %param.3) | copy-start | bytes 18436
  170.7 8.5 %collective-permute-start = (f32[1,8,6,32]{3,1,0,2:T(8,128)S(1)}, f32[1,8,6,32]{3,1,0,2:T(8,128)S(1)}, u32[]{:S(2)}, u32[]{:S(2)}) collective-permute-start(f32[1,8,6,32]{3,1,0,2:T(8,128)S(1)} %get-tuple-element.25), channel_id=1, source_target_pairs={{0,8},{8,16},{16,24},{24,32},{32,40},{40,48},{48,56},{56,64},{64,7... | collective-permute-start | bytes 18440 | tf_op jit(solution)/shard_map/ppermute | solution.py:19
  172.7 7.3 %collective-permute-start.1 = (f32[1,8,6,32]{3,1,0,2:T(8,128)S(1)}, f32[1,8,6,32]{3,1,0,2:T(8,128)S(1)}, u32[]{:S(2)}, u32[]{:S(2)}) collective-permute-start(f32[1,8,6,32]{3,1,0,2:T(8,128)S(1)} %get-tuple-element.26), channel_id=1, source_target_pairs={{8,0},{16,8},{24,16},{32,24},{40,32},{48,40},{56,48},{64,56},{72,6... | collective-permute-start | bytes 18440 | tf_op jit(solution)/shard_map/ppermute | solution.py:20
  180.1 7.2 %collective-permute-start.2 = (f32[4,8,6,1]{3,1,0,2:T(8,128)S(1)}, f32[4,8,6,1]{3,1,0,2:T(8,128)S(1)}, u32[]{:S(2)}, u32[]{:S(2)}) collective-permute-start(f32[4,8,6,1]{3,1,0,2:T(8,128)S(1)} %get-tuple-element.16), channel_id=1, source_target_pairs={{0,1},{1,2},{2,3},{3,4},{4,5},{5,6},{6,7},{8,9},{9,10},{10,11},{11... | collective-permute-start | bytes 2312 | tf_op jit(solution)/shard_map/ppermute | solution.py:19
  184.1 13.6 %collective-permute-start.3 = (f32[4,8,6,1]{3,1,0,2:T(8,128)S(1)}, f32[4,8,6,1]{3,1,0,2:T(8,128)S(1)}, u32[]{:S(2)}, u32[]{:S(2)}) collective-permute-start(f32[4,8,6,1]{3,1,0,2:T(8,128)S(1)} %get-tuple-element.17), channel_id=1, source_target_pairs={{1,0},{2,1},{3,2},{4,3},{5,4},{6,5},{7,6},{9,8},{10,9},{11,10},{12... | collective-permute-start | bytes 2312 | tf_op jit(solution)/shard_map/ppermute | solution.py:20
Sparse Core Ops, SparseCore 0:
  10.2 123.7 all-gather.1
where the time goes:
time: 206 us
  waiting for transfers between devices  137 us (67%)
  blocking collectives  17.5 us (8%)
  between operations  14.3 us (7%)
  starting transfers between devices  13.6 us (7%)
  matrix products  11.2 us (5%)
  other arithmetic  9 us (4%)
  local copies, waits for them, and re-layouts  3.17 us (2%)
    all_gather x1, waiting for transfers between devices, on_device(): shard_piece = lax.all_gather(amplitudes, 'ky', axis=1, tiled=True)  124 us
    all_to_all x1, blocking collectives, on_device(): lax.all_to_all(partial_field, 'gz', split_axis=3, concat_axis=1, tiled=True)  17.5 us
    ppermute x2, waiting for transfers between devices, extended(): after = lax.ppermute(initial, axis, down)  11.1 us
    dot_general x1, matrix products, x_section(): jnp.dot(flat_modes, table_x, precision=lax.Precision.HIGHEST, preferred_e...  10.6 us
    ppermute x2, starting transfers between devices, extended(): after = lax.ppermute(initial, axis, down)  7.67 us
    ppermute x2, starting transfers between devices, extended(): before = lax.ppermute(last, axis, up)  5.9 us
  transfers between devices with their start and end apart: 5, of which 4 were waited for; matrix products, arithmetic and copies ran while one was open for 1% of the time, Pallas kernels for 0%

commit v1 on v0

v1 whole, which is shorter than its diff:
```python
import jax
import jax.numpy as jnp
import ml_dtypes
import numpy as np
from jax import lax
from jax.experimental import pallas as pl
from jax.experimental.pallas import tpu as pltpu
from jax.sharding import PartitionSpec as P

band_factor = 16.0
cell_height = 0.125
time_step = 0.05
viscosity = 0.02
lanes = 128
f32 = jnp.float32


def split(x):
    high = x.astype(jnp.bfloat16)
    return high, (x - high.astype(f32)).astype(jnp.bfloat16)


def split_table(table):
    high = table.astype(np.float32).astype(ml_dtypes.bfloat16)
    return high, (table - high.astype(np.float64)).astype(np.float32).astype(ml_dtypes.bfloat16)


def x_tables(kx_count, zone_x, x_tile):
    cells = np.arange(zone_x).reshape(-1, x_tile).T.reshape(-1)
    turns = np.outer(cells * 2 + 1, np.arange(kx_count)) % int(2 * band_factor * kx_count)
    phase = turns * (2.0 * np.pi / (2 * band_factor * kx_count))
    return split_table(np.concatenate([np.cos(phase), np.sin(phase)], axis=0))


def y_tables(wave_count, zone_y, y_tile, wave_local, height):
    tiles = zone_y // y_tile
    cells = np.arange(tiles)[:, None] * y_tile + np.arange(y_tile + 2)[None] - 1
    inside = (cells >= 0) & (cells < zone_y)
    rows = np.arange(wave_count).reshape(-1, wave_local).T.reshape(-1) - wave_count // 2
    turns = (cells[..., None] * 2 + 1) * rows % int(2 * band_factor * wave_count)
    phase = turns * (2.0 * np.pi / (2 * band_factor * wave_count))
    table = np.concatenate([np.cos(phase), -np.sin(phase)], axis=-1) * inside[..., None]
    table = np.pad(table, ((0, 0), (0, height - table.shape[1]), (0, 0)))
    return np.concatenate(split_table(table), axis=1)


def dot_nt(a, b):
    return lax.dot_general(a, b, (((1,), (1,)), ((), ())), preferred_element_type=f32)


def x_kernel(ky_groups, level_count, wave_count, amplitudes, table_hi, table_lo, out):
    wave_local, kx_count = amplitudes.shape[1:]
    per_row = 3 * level_count
    first = lax.axis_index("ky") * wave_local
    rows = (first + lax.broadcasted_iota(jnp.int32, (wave_local, kx_count), 0)).astype(f32)
    step_y = 2.0 * np.pi / (band_factor * wave_count)
    step_x = 2.0 * np.pi / (band_factor * kx_count)
    along_y = (rows - wave_count / 2.0) * step_y
    columns = lax.broadcasted_iota(jnp.int32, (wave_local, kx_count), 1).astype(f32)
    along_x = columns * step_x
    magnitude = jnp.sqrt(along_x * along_x + along_y * along_y)
    shape = (level_count, kx_count)
    depths = -(lax.broadcasted_iota(jnp.int32, shape, 0).astype(f32) + 0.5) * cell_height
    kx = along_x[0:1]
    parts_re, parts_im = [], []
    for n in range(wave_local):
        k = magnitude[n : n + 1]
        ky = along_y[n : n + 1]
        decay = jnp.exp(jnp.broadcast_to(k, shape) * depths)
        re = decay * amplitudes[0, n : n + 1]
        im = decay * amplitudes[1, n : n + 1]
        parts_re += [-kx * im, -ky * im, k * re]
        parts_im += [kx * re, ky * re, k * im]
    modes_hi, modes_lo = split(jnp.concatenate(parts_re + parts_im, axis=0))
    product = dot_nt(table_hi[...], modes_hi)
    product += dot_nt(table_hi[...], modes_lo) + dot_nt(table_lo[...], modes_hi)
    half = product.shape[0] // 2
    by_cos, by_sin = product[:half], product[half:]
    middle = wave_local * per_row
    turned = jnp.concatenate([-by_sin[:, middle:], by_sin[:, :middle]], axis=1)
    field = by_cos + turned
    even, odd = field[:ky_groups], field[ky_groups:]
    width = field.shape[1] // lanes
    chunk = 4 * width
    for j in range(width):
        cut = slice(lanes * j, lanes * (j + 1))
        out[pl.ds(j + chunk, ky_groups - 1, stride=chunk), :] = odd[: ky_groups - 1, cut]
        out[pl.ds(j, 1), :] = jnp.zeros((1, lanes), f32)
        out[pl.ds(j + width, ky_groups, stride=chunk), :] = even[:, cut]
        out[pl.ds(j + 2 * width, ky_groups, stride=chunk), :] = odd[:, cut]
        out[pl.ds(j + 3 * width, ky_groups - 1, stride=chunk), :] = even[1:, cut]
        out[pl.ds((ky_groups - 1) * chunk + j + 3 * width, 1), :] = jnp.zeros((1, lanes), f32)


def face(a, b):
    return [0.5 * (p + q) for p, q in zip(a, b)]


def flux(inc, comp, normal):
    total = inc[normal] + comp[normal]
    return [total * comp[c] + comp[normal] * inc[c] for c in range(3)]


def y_kernel(ky_groups, wave_local, height, received, table, comp, x_low, x_high, y_low, y_high, incident, predicted, padded):
    level_count, y_tile = comp.shape[2:]
    per_row = 3 * level_count
    width = 2 * wave_local * per_row // lanes
    chunk = 4 * width
    cols = [[received[pl.ds(k * width + t, ky_groups, stride=chunk), :] for t in range(width)] for k in range(4)]
    lane = lax.broadcasted_iota(jnp.int32, (ky_groups, lanes), 1)
    blocks = []
    for b in range(2 * wave_local):
        first, offset = divmod(b * per_row, lanes)
        block = None
        for k in range(4):
            at = k * per_row
            shift = (at - offset) % lanes
            piece = pltpu.roll(cols[k][first], shift, axis=1) if shift else cols[k][first]
            if offset + per_row > lanes:
                rest = pltpu.roll(cols[k][first + 1], shift, axis=1) if shift else cols[k][first + 1]
                piece = jnp.where(lane < at + lanes - offset, piece, rest)
            block = piece if block is None else jnp.where(lane < at, block, piece)
        blocks.append(block)
    modes_hi, modes_lo = split(jnp.concatenate(blocks, axis=0))
    both = jnp.dot(table[...], modes_hi, preferred_element_type=f32)
    field = both[:height] + both[height:]
    field += jnp.dot(table[:height], modes_lo, preferred_element_type=f32)
    field = jnp.concatenate([field, jnp.zeros((lanes - height, lanes), f32)], axis=0).T
    inc = [
        [field[(k * 3 + c) * level_count : (k * 3 + c + 1) * level_count] for c in range(3)]
        for k in range(4)
    ]
    padded[...] = jnp.zeros_like(padded)
    for c in range(3):
        padded[0, c, :, 1 : y_tile + 1] = x_low[1, c]
        padded[3, c, :, 1 : y_tile + 1] = x_high[0, c]
        for x in range(2):
            padded[x + 1, c, :, 1 : y_tile + 1] = comp[x, c]
            padded[x + 1, c, :, 0:1] = y_low[x, c, :, y_tile - 1 : y_tile]
            padded[x + 1, c, :, y_tile + 1 : y_tile + 2] = y_high[x, c, :, 0:1]
    cells = [[padded[k, c] for c in range(3)] for k in range(4)]
    level = lax.broadcasted_iota(jnp.int32, (level_count, lanes), 0)

    def below(v):
        return jnp.where(level == 0, 0.0, pltpu.roll(v, 1, axis=0))

    def above(v):
        return jnp.where(level == level_count - 1, 0.0, pltpu.roll(v, level_count - 1, axis=0))

    def before(v):
        return pltpu.roll(v, 1, axis=1)

    def after(v):
        return pltpu.roll(v, lanes - 1, axis=1)

    x_flux = [flux(face(inc[k], inc[k + 1]), face(cells[k], cells[k + 1]), 0) for k in range(3)]
    for x in range(2):
        own_inc, own = inc[x + 1], cells[x + 1]
        inc_before, own_before = [before(v) for v in own_inc], [before(v) for v in own]
        y_lower = flux(face(inc_before, own_inc), face(own_before, own), 1)
        inc_below, own_below = [below(v) for v in own_inc], [below(v) for v in own]
        inc_above, own_above = [above(v) for v in own_inc], [above(v) for v in own]
        z_lower = flux(face(inc_below, own_inc), face(own_below, own), 2)
        z_upper = flux(face(own_inc, inc_above), face(own, own_above), 2)
        for c in range(3):
            twice = 2.0 * own[c]
            tendency = -(x_flux[x + 1][c] - x_flux[x][c])
            tendency += viscosity * (cells[x][c] + cells[x + 2][c] - twice)
            tendency -= after(y_lower[c]) - y_lower[c]
            tendency += viscosity * (own_before[c] + after(own[c]) - twice)
            tendency -= (z_upper[c] - z_lower[c]) / cell_height
            tendency += viscosity * (own_below[c] + own_above[c] - twice) / cell_height**2
            result = own[c] + time_step * tendency
            incident[x, c] = own_inc[c][:, 1 : y_tile + 1]
            predicted[x, c] = result[:, 1 : y_tile + 1]


def on_device(amplitudes, complementary):
    x_tile, level_count, _, y_tile = complementary.shape
    ky_groups, gz_groups = lax.axis_size("ky"), lax.axis_size("gz")
    wave_local, kx_count = amplitudes.shape[1:]
    wave_count = wave_local * ky_groups
    height = -(-(y_tile + 2) // 8) * 8
    chunk = 4 * 2 * wave_local * 3 * level_count // lanes
    table_hi, table_lo = x_tables(kx_count, x_tile * ky_groups, x_tile)
    table_y = y_tables(wave_count, y_tile * gz_groups, y_tile, wave_local, height)
    vmem = pl.BlockSpec(memory_space=pltpu.VMEM)

    def x_call(*refs):
        x_kernel(ky_groups, level_count, wave_count, *refs)

    def y_call(*refs):
        y_kernel(ky_groups, wave_local, height, *refs)

    with jax.named_scope("x_transform"):
        sent = pl.pallas_call(
            x_call,
            out_shape=jax.ShapeDtypeStruct((ky_groups * chunk, lanes), f32),
            in_specs=[vmem] * 3,
            out_specs=vmem,
            compiler_params=pltpu.CompilerParams(vmem_limit_bytes=48 * 2**20),
            name="x_transform",
        )(amplitudes, jnp.asarray(table_hi), jnp.asarray(table_lo))
    comp = jnp.transpose(complementary, (0, 2, 1, 3))
    halos = []
    for axis, size in (("ky", ky_groups), ("gz", gz_groups)):
        up = [(i, i + 1) for i in range(size - 1)]
        halos.append(lax.ppermute(comp, axis, up))
        halos.append(lax.ppermute(comp, axis, [(j, i) for i, j in up]))
    received = lax.all_to_all(sent.reshape(ky_groups, chunk, lanes), "ky", 0, 0)
    table = lax.dynamic_index_in_dim(jnp.asarray(table_y), lax.axis_index("gz"), 0, keepdims=False)
    result = jax.ShapeDtypeStruct(comp.shape, f32)
    with jax.named_scope("y_transform_and_step"):
        incident, predicted = pl.pallas_call(
            y_call,
            out_shape=(result, result),
            in_specs=[vmem] * 7,
            out_specs=(vmem, vmem),
            scratch_shapes=[pltpu.VMEM((4, 3, level_count, lanes), f32)],
            compiler_params=pltpu.CompilerParams(vmem_limit_bytes=48 * 2**20),
            name="y_transform",
        )(received.reshape(ky_groups * chunk, lanes), table, comp, *halos)
    back = (0, 2, 1, 3)
    return jnp.transpose(incident, back), jnp.transpose(predicted, back)


def solution(mesh):
    placed = (P(None, "ky", None), P("ky", None, None, "gz"))
    return jax.shard_map(
        on_device,
        mesh=mesh,
        in_specs=placed,
        out_specs=(P("ky", None, None, "gz"), P("ky", None, None, "gz")),
        check_vma=False,
    )
```

time: 206 us -> 46.5 us (0.23)
  waiting for transfers between devices: 137 us -> 8.81 us
  blocking collectives: 17.5 us -> 0 us
  starting transfers between devices: 13.6 us -> 28.9 us
  between operations: 14.3 us -> 0.74 us
  matrix products: 11.2 us -> 0 us
  other arithmetic: 9 us -> 0 us
  Pallas kernels: 0 us -> 2.91 us
    all_gather x1 -> x0, waiting for transfers between devices: 124 us -> none  [on_device(): shard_piece = lax.all_gather(amplitudes, 'ky', axis=1, tiled=True)]
    all_to_all x1 -> x0, blocking collectives: 17.5 us -> none  [on_device(): lax.all_to_all(partial_field, 'gz', split_axis=3, concat_axis=1, tiled=True)]
    all_to_all x0 -> x1, starting transfers between devices: none -> 14.4 us  [on_device(): received = lax.all_to_all(sent.reshape(ky_groups, chunk, lanes), 'ky', 0, 0)]
    dot_general x2 -> x0, matrix products: 11.2 us -> none  [the longest x1 10.6 us: x_section(): jnp.dot(flat_modes, table_x, precision=lax.Precision.HIGHEST, preferred_e...]
    another operation x3 -> x0, other arithmetic: 5.52 us -> none  [the longest x1 3.23 us: x_section(): jnp.stack([-factor_x * scaled_im, -factor_y * scaled_im, factor_k * scale...]
    ppermute x4, waiting for transfers between devices: 12.3 us -> 7.47 us  [the longest x2 7.47 us: on_device(): halos.append(lax.ppermute(comp, axis, [(j, i) for i, j in up]))]
    pallas_call x0 -> x2, Pallas kernels: none -> 2.91 us  [the longest x1 1.75 us: on_device(): pl.pallas_call(y_call, out_shape=(result, result), in_specs=[vmem] * 7, o...]
    cos x2 -> x0, other arithmetic: 2.09 us -> none  [the longest x1 1.89 us: y_section(): table_y = jnp.concatenate([jnp.cos(phase_y), jnp.sin(phase_y)], axis=0)]
  transfers between devices with their start and end apart: 5 -> 5, of which waited for: 4 -> 2; matrix products, arithmetic and copies ran while one was open for 1% -> 2% of each run, Pallas kernels for 0% -> 0%
where the time goes in v1:
time: 46.5 us; the launch traced here: 46.1 us
  starting transfers between devices  28.9 us (62%)
  waiting for transfers between devices  8.81 us (19%)
  local copies, waits for them, and re-layouts  4.72 us (10%)
  Pallas kernels  2.91 us (6%)
  between operations  0.74 us (2%)
    all_to_all x1, starting transfers between devices, on_device(): received = lax.all_to_all(sent.reshape(ky_groups, chunk, lanes), 'ky', 0, 0)  14.4 us
    ppermute x2, starting transfers between devices, on_device(): halos.append(lax.ppermute(comp, axis, [(j, i) for i, j in up]))  7.54 us
    ppermute x2, waiting for transfers between devices, on_device(): halos.append(lax.ppermute(comp, axis, [(j, i) for i, j in up]))  7.47 us
    ppermute x2, starting transfers between devices, on_device(): halos.append(lax.ppermute(comp, axis, up))  7.01 us
    unnamed x8, local copies, waits for them, and re-layouts  2.92 us
    pallas_call x1, Pallas kernels, on_device(): pl.pallas_call(y_call, out_shape=(result, result), in_specs=[vmem] * 7, o...  1.75 us
    all_to_all x1, waiting for transfers between devices, on_device(): received = lax.all_to_all(sent.reshape(ky_groups, chunk, lanes), 'ky', 0, 0)  1.33 us
    pallas_call x1, Pallas kernels, on_device(): pl.pallas_call(x_call, out_shape=jax.ShapeDtypeStruct((ky_groups * chunk,...  1.16 us
  transfers between devices with their start and end apart: 5, of which 2 were waited for; matrix products, arithmetic and copies ran while one was open for 2% of the time, Pallas kernels for 0%

profile of v1, /device:TPU:14, one launch (start us, length us, event | category | flops | bytes accessed | tf_op | source)
XLA Modules:
  0.0 46.1 jit_solution(15637262867139894474)
XLA Ops:
  0.6 0.0 copy-start
  0.6 1.0 %copy-done = bf16[256,1024]{1,0:T(8,128)(2,1)S(1)} copy-done((bf16[256,1024]{1,0:T(8,128)(2,1)S(1)}, bf16[256,1024]{1,0:T(8,128)(2,1)}, u32[]{:S(2)}) %copy-start) | copy-done | bytes 524312
  1.7 0.0 copy-start.1
  1.7 1.0 %copy-done.1 = bf16[256,1024]{1,0:T(8,128)(2,1)S(1)} copy-done((bf16[256,1024]{1,0:T(8,128)(2,1)S(1)}, bf16[256,1024]{1,0:T(8,128)(2,1)}, u32[]{:S(2)}) %copy-start.1) | copy-done | bytes 524312
  2.7 0.0 copy-start.2
  2.7 0.8 %copy-done.2 = f32[2,8,1024]{2,1,0:T(8,128)S(1)} copy-done((f32[2,8,1024]{2,1,0:T(8,128)S(1)}, f32[2,8,1024]{2,1,0:T(8,128)}, u32[]{:S(2)}) %copy-start.2) | copy-done | bytes 65560
  3.6 1.2 %x_transform.1 = f32[768,128]{1,0:T(8,128)S(1)} custom-call(f32[2,8,1024]{2,1,0:T(8,128)S(1)} %copy-done.2, bf16[256,1024]{1,0:T(8,128)(2,1)S(1)} %copy-done, bf16[256,1024]{1,0:T(8,128)(2,1)S(1)} %copy-done.1), custom_call_target="tpu_custom_call" | custom-call | tf_op jit(solution)/shard_map/x_transform/x_transform/pallas_call | solution.py:196
  4.7 0.0 copy-start.3
  4.7 0.8 %reshape.10 = f32[64,12,128]{2,1,0:T(8,128)} reshape(f32[768,128]{1,0:T(8,128)S(1)} %x_transform.1) | data formatting | bytes 786432 | tf_op jit(solution)/shard_map/reshape | solution.py:210
  5.6 14.4 %all-to-all-start = ((f32[64,12,128]{2,1,0:T(8,128)}), f32[64,12,128]{2,1,0:T(8,128)S(1)}, u32[]{:S(2)}, u32[]{:S(2)}) async-start(f32[64,12,128]{2,1,0:T(8,128)} %reshape.10), calls=%async_computation | async-start | bytes 1048576 | tf_op jit(solution)/shard_map/all_to_all | solution.py:210
  19.9 0.0 copy-done.3
  19.9 2.1 %collective-permute-start = (f32[2,3,8,32]{3,2,1,0:T(8,128)S(1)}, f32[2,3,8,32]{3,2,1,0:T(8,128)S(1)}, u32[]{:S(2)}, u32[]{:S(2)}) collective-permute-start(f32[2,3,8,32]{3,2,1,0:T(8,128)S(1)} %bitcast.5), channel_id=1, source_target_pairs={{0,8},{8,16},{16,24},{24,32},{32,40},{40,48},{48,56},{56,64},{64,7... | collective-permute-start | bytes 18440 | tf_op jit(solution)/shard_map/ppermute | solution.py:208
  22.0 5.6 %collective-permute-start.1 = (f32[2,3,8,32]{3,2,1,0:T(8,128)S(1)}, f32[2,3,8,32]{3,2,1,0:T(8,128)S(1)}, u32[]{:S(2)}, u32[]{:S(2)}) collective-permute-start(f32[2,3,8,32]{3,2,1,0:T(8,128)S(1)} %bitcast.6), channel_id=1, source_target_pairs={{8,0},{16,8},{24,16},{32,24},{40,32},{48,40},{56,48},{64,56},{72,6... | collective-permute-start | bytes 18440 | tf_op jit(solution)/shard_map/ppermute | solution.py:209
  27.6 5.0 %collective-permute-start.2 = (f32[2,3,8,32]{3,2,1,0:T(8,128)S(1)}, f32[2,3,8,32]{3,2,1,0:T(8,128)S(1)}, u32[]{:S(2)}, u32[]{:S(2)}) collective-permute-start(f32[2,3,8,32]{3,2,1,0:T(8,128)S(1)} %bitcast.7), channel_id=1, source_target_pairs={{0,1},{1,2},{2,3},{3,4},{4,5},{5,6},{6,7},{8,9},{9,10},{10,11},{11... | collective-permute-start | bytes 18440 | tf_op jit(solution)/shard_map/ppermute | solution.py:208
  32.6 1.9 %collective-permute-start.3 = (f32[2,3,8,32]{3,2,1,0:T(8,128)S(1)}, f32[2,3,8,32]{3,2,1,0:T(8,128)S(1)}, u32[]{:S(2)}, u32[]{:S(2)}) collective-permute-start(f32[2,3,8,32]{3,2,1,0:T(8,128)S(1)} %bitcast.8), channel_id=1, source_target_pairs={{1,0},{2,1},{3,2},{4,3},{5,4},{6,5},{7,6},{9,8},{10,9},{11,10},{12... | collective-permute-start | bytes 18440 | tf_op jit(solution)/shard_map/ppermute | solution.py:209
  34.5 0.9 %dynamic-slice_bitcast_fusion.refs_1_ = bf16[80,1024]{1,0:T(8,128)(2,1)S(1)} fusion(bf16[8,80,1024]{2,1,0:T(8,128)(2,1)} %constant.18.clone, s32[]{:T(128)S(6)} %select_n.4), kind=kLoop, calls=%fused_computation | loop fusion | bytes 327684 | tf_op jit(solution)/shard_map/jit(dynamic_index_in_dim)/squeeze | solution.py:211
  35.5 1.3 %all-to-all-done = f32[64,12,128]{2,1,0:T(8,128)S(1)} async-done(((f32[64,12,128]{2,1,0:T(8,128)}), f32[64,12,128]{2,1,0:T(8,128)S(1)}, u32[]{:S(2)}, u32[]{:S(2)}) %all-to-all-start) | async-done | bytes 393248 | tf_op jit(solution)/shard_map/all_to_all | solution.py:210
  36.8 0.0 collective-permute-done.refs_3_
  36.8 0.0 collective-permute-done.1.refs_4_
  36.9 0.0 collective-permute-done.2.refs_5_
  36.9 7.5 %collective-permute-done.3.refs_6_ = f32[2,3,8,32]{3,2,1,0:T(8,128)S(1)} collective-permute-done((f32[2,3,8,32]{3,2,1,0:T(8,128)S(1)}, f32[2,3,8,32]{3,2,1,0:T(8,128)S(1)}, u32[]{:S(2)}, u32[]{:S(2)}) %collective-permute-start.3) | collective-permute-done | bytes 6176 | tf_op jit(solution)/shard_map/ppermute | solution.py:209
  44.3 1.7 %y_transform.1 = (f32[2,3,8,32]{3,2,1,0:T(8,128)}, f32[2,3,8,32]{3,2,1,0:T(8,128)}) custom-call(f32[768,128]{1,0:T(8,128)S(1)} %reshape.11.refs_0_, bf16[80,1024]{1,0:T(8,128)(2,1)S(1)} %dynamic-slice_bitcast_fusion.refs_1_, f32[2,3,8,32]{3,2,1,0:T(8,128)S(1)} %bitcast.9, f32[2,3,8,32]{3,2,1,0:T(8,128)S(1)} %collective-permute-done.refs_3_, ...), custom_call_target="tpu_custom_call" | custom-call | tf_op jit(solution)/shard_map/y_transform_and_step/y_transform/pallas_call | solution.py:214
  (1 shorter events, 0.0 us)
Async XLA Ops:
  0.6 1.0 %copy-start = (bf16[256,1024]{1,0:T(8,128)(2,1)S(1)}, bf16[256,1024]{1,0:T(8,128)(2,1)}, u32[]{:S(2)}) copy-start(bf16[256,1024]{1,0:T(8,128)(2,1)} %constant.16.clone.refs_1_) | copy-start | bytes 1572868
  1.7 1.0 %copy-start.1 = (bf16[256,1024]{1,0:T(8,128)(2,1)S(1)}, bf16[256,1024]{1,0:T(8,128)(2,1)}, u32[]{:S(2)}) copy-start(bf16[256,1024]{1,0:T(8,128)(2,1)} %constant.17.clone.refs_2_) | copy-start | bytes 1572868
  2.7 0.8 %copy-start.2 = (f32[2,8,1024]{2,1,0:T(8,128)S(1)}, f32[2,8,1024]{2,1,0:T(8,128)}, u32[]{:S(2)}) copy-start(f32[2,8,1024]{2,1,0:T(8,128)} %refs_0_.1) | copy-start | bytes 196612
  4.7 15.2 %copy-start.3 = (f32[2,8,3,32]{3,1,2,0:T(8,128)S(1)}, f32[2,8,3,32]{3,1,2,0:T(8,128)}, u32[]{:S(2)}) copy-start(f32[2,8,3,32]{3,1,2,0:T(8,128)} %param.6) | copy-start | bytes 18436
  5.6 31.2 %all-to-all-start = ((f32[64,12,128]{2,1,0:T(8,128)}), f32[64,12,128]{2,1,0:T(8,128)S(1)}, u32[]{:S(2)}, u32[]{:S(2)}) async-start(f32[64,12,128]{2,1,0:T(8,128)} %reshape.10), calls=%async_computation | async-start | bytes 1048576 | tf_op jit(solution)/shard_map/all_to_all | solution.py:210
  19.9 16.9 %collective-permute-start = (f32[2,3,8,32]{3,2,1,0:T(8,128)S(1)}, f32[2,3,8,32]{3,2,1,0:T(8,128)S(1)}, u32[]{:S(2)}, u32[]{:S(2)}) collective-permute-start(f32[2,3,8,32]{3,2,1,0:T(8,128)S(1)} %bitcast.5), channel_id=1, source_target_pairs={{0,8},{8,16},{16,24},{24,32},{32,40},{40,48},{48,56},{56,64},{64,7... | collective-permute-start | bytes 18440 | tf_op jit(solution)/shard_map/ppermute | solution.py:208
  22.0 14.8 %collective-permute-start.1 = (f32[2,3,8,32]{3,2,1,0:T(8,128)S(1)}, f32[2,3,8,32]{3,2,1,0:T(8,128)S(1)}, u32[]{:S(2)}, u32[]{:S(2)}) collective-permute-start(f32[2,3,8,32]{3,2,1,0:T(8,128)S(1)} %bitcast.6), channel_id=1, source_target_pairs={{8,0},{16,8},{24,16},{32,24},{40,32},{48,40},{56,48},{64,56},{72,6... | collective-permute-start | bytes 18440 | tf_op jit(solution)/shard_map/ppermute | solution.py:209
  27.6 9.2 %collective-permute-start.2 = (f32[2,3,8,32]{3,2,1,0:T(8,128)S(1)}, f32[2,3,8,32]{3,2,1,0:T(8,128)S(1)}, u32[]{:S(2)}, u32[]{:S(2)}) collective-permute-start(f32[2,3,8,32]{3,2,1,0:T(8,128)S(1)} %bitcast.7), channel_id=1, source_target_pairs={{0,1},{1,2},{2,3},{3,4},{4,5},{5,6},{6,7},{8,9},{9,10},{10,11},{11... | collective-permute-start | bytes 18440 | tf_op jit(solution)/shard_map/ppermute | solution.py:208
  32.6 11.7 %collective-permute-start.3 = (f32[2,3,8,32]{3,2,1,0:T(8,128)S(1)}, f32[2,3,8,32]{3,2,1,0:T(8,128)S(1)}, u32[]{:S(2)}, u32[]{:S(2)}) collective-permute-start(f32[2,3,8,32]{3,2,1,0:T(8,128)S(1)} %bitcast.8), channel_id=1, source_target_pairs={{1,0},{2,1},{3,2},{4,3},{5,4},{6,5},{7,6},{9,8},{10,9},{11,10},{12... | collective-permute-start | bytes 18440 | tf_op jit(solution)/shard_map/ppermute | solution.py:209

commit v2 on v1

--- a/solution.py
+++ b/solution.py
@@ -25,11 +25,12 @@
     return high, (table - high.astype(np.float64)).astype(np.float32).astype(ml_dtypes.bfloat16)
 
 
-def x_tables(kx_count, zone_x, x_tile):
-    cells = np.arange(zone_x).reshape(-1, x_tile).T.reshape(-1)
-    turns = np.outer(cells * 2 + 1, np.arange(kx_count)) % int(2 * band_factor * kx_count)
+def x_tables(kx_count):
+    near = np.arange(16).reshape(8, 2).T.reshape(-1) * 2 + 1
+    halves = np.concatenate([near, 32 * np.arange(8)])
+    turns = np.outer(halves, np.arange(kx_count)) % int(2 * band_factor * kx_count)
     phase = turns * (2.0 * np.pi / (2 * band_factor * kx_count))
-    return split_table(np.concatenate([np.cos(phase), np.sin(phase)], axis=0))
+    return np.stack([np.cos(phase), np.sin(phase)]).astype(np.float32)
 
 
 def y_tables(wave_count, zone_y, y_tile, wave_local, height):
@@ -48,11 +49,17 @@
     return lax.dot_general(a, b, (((1,), (1,)), ((), ())), preferred_element_type=f32)
 
 
-def x_kernel(ky_groups, level_count, wave_count, amplitudes, table_hi, table_lo, out):
+def x_kernel(ky_groups, level_count, wave_count, amplitudes, tables, out, modes, table, sems):
+    copies = [
+        pltpu.make_async_copy(source, target, sems.at[i])
+        for i, (source, target) in enumerate(((tables, table), (amplitudes, modes)))
+    ]
+    for copy in copies:
+        copy.start()
     wave_local, kx_count = amplitudes.shape[1:]
     per_row = 3 * level_count
-    first = lax.axis_index("ky") * wave_local
-    rows = (first + lax.broadcasted_iota(jnp.int32, (wave_local, kx_count), 0)).astype(f32)
+    me = lax.axis_index("ky")
+    rows = (me * wave_local + lax.broadcasted_iota(jnp.int32, (wave_local, kx_count), 0)).astype(f32)
     step_y = 2.0 * np.pi / (band_factor * wave_count)
     step_x = 2.0 * np.pi / (band_factor * kx_count)
     along_y = (rows - wave_count / 2.0) * step_y
@@ -62,18 +69,28 @@
     shape = (level_count, kx_count)
     depths = -(lax.broadcasted_iota(jnp.int32, shape, 0).astype(f32) + 0.5) * cell_height
     kx = along_x[0:1]
+    decays = [jnp.exp(jnp.broadcast_to(magnitude[n : n + 1], shape) * depths) for n in range(wave_local)]
+    copies[0].wait()
+    cos_rows, sin_rows = [], []
+    for e in range(2):
+        cos_near, sin_near = table[0, 8 * e : 8 * e + 8], table[1, 8 * e : 8 * e + 8]
+        for i in range(ky_groups // 8):
+            cos_far, sin_far = table[0, 16 + i : 17 + i], table[1, 16 + i : 17 + i]
+            cos_rows.append(cos_near * cos_far - sin_near * sin_far)
+            sin_rows.append(sin_near * cos_far + cos_near * sin_far)
+    table_hi, table_lo = split(jnp.concatenate(cos_rows + sin_rows, axis=0))
+    copies[1].wait()
     parts_re, parts_im = [], []
     for n in range(wave_local):
         k = magnitude[n : n + 1]
         ky = along_y[n : n + 1]
-        decay = jnp.exp(jnp.broadcast_to(k, shape) * depths)
-        re = decay * amplitudes[0, n : n + 1]
-        im = decay * amplitudes[1, n : n + 1]
+        re = decays[n] * modes[0, n : n + 1]
+        im = decays[n] * modes[1, n : n + 1]
         parts_re += [-kx * im, -ky * im, k * re]
         parts_im += [kx * re, ky * re, k * im]
     modes_hi, modes_lo = split(jnp.concatenate(parts_re + parts_im, axis=0))
-    product = dot_nt(table_hi[...], modes_hi)
-    product += dot_nt(table_hi[...], modes_lo) + dot_nt(table_lo[...], modes_hi)
+    product = dot_nt(table_hi, modes_hi)
+    product += dot_nt(table_hi, modes_lo) + dot_nt(table_lo, modes_hi)
     half = product.shape[0] // 2
     by_cos, by_sin = product[:half], product[half:]
     middle = wave_local * per_row
@@ -101,9 +118,9 @@
     return [total * comp[c] + comp[normal] * inc[c] for c in range(3)]
 
 
-def y_kernel(ky_groups, wave_local, height, received, table, comp, x_low, x_high, y_low, y_high, incident, predicted, padded):
-    level_count, y_tile = comp.shape[2:]
-    per_row = 3 * level_count
+def y_kernel(ky_groups, wave_local, height, received, table, comp, y_out, y_in, x_out, x_in, incident, predicted, padded):
+    per_row, y_tile = comp.shape[1:]
+    level_count = per_row // 3
     width = 2 * wave_local * per_row // lanes
     chunk = 4 * width
     cols = [[received[pl.ds(k * width + t, ky_groups, stride=chunk), :] for t in range(width)] for k in range(4)]
@@ -131,14 +148,16 @@
         for k in range(4)
     ]
     padded[...] = jnp.zeros_like(padded)
-    for c in range(3):
-        padded[0, c, :, 1 : y_tile + 1] = x_low[1, c]
-        padded[3, c, :, 1 : y_tile + 1] = x_high[0, c]
-        for x in range(2):
-            padded[x + 1, c, :, 1 : y_tile + 1] = comp[x, c]
-            padded[x + 1, c, :, 0:1] = y_low[x, c, :, y_tile - 1 : y_tile]
-            padded[x + 1, c, :, y_tile + 1 : y_tile + 2] = y_high[x, c, :, 0:1]
-    cells = [[padded[k, c] for c in range(3)] for k in range(4)]
+    x_even = lax.axis_index("ky") % 2 == 0
+    y_even = lax.axis_index("gz") % 2 == 0
+    inner = slice(1, y_tile + 1)
+    padded[0, :, inner] = jnp.where(x_even, x_out[1], x_in[1])
+    padded[3, :, inner] = jnp.where(x_even, x_in[0], x_out[0])
+    for x in range(2):
+        padded[x + 1, :, inner] = comp[x]
+        padded[x + 1, :, 0:1] = jnp.where(y_even, y_out[x], y_in[x])[:, y_tile - 1 : y_tile]
+        padded[x + 1, :, y_tile + 1 : y_tile + 2] = jnp.where(y_even, y_in[x], y_out[x])[:, 0:1]
+    cells = [[padded[k, c * level_count : (c + 1) * level_count] for c in range(3)] for k in range(4)]
     level = lax.broadcasted_iota(jnp.int32, (level_count, lanes), 0)
 
     def below(v):
@@ -175,6 +194,15 @@
             predicted[x, c] = result[:, 1 : y_tile + 1]
 
 
+def swaps(size, first):
+    pairs = [(i, i + 1) for i in range(first, size - 1, 2)]
+    return pairs + [(j, i) for i, j in pairs]
+
+
+PAIRS = (("ky", 0), ("ky", 1), ("gz", 0), ("gz", 1))
+ORDER = (("gz", 1), ("gz", 0), ("ky", 1), ("ky", 0))
+
+
 def on_device(amplitudes, complementary):
     x_tile, level_count, _, y_tile = complementary.shape
     ky_groups, gz_groups = lax.axis_size("ky"), lax.axis_size("gz")
@@ -182,9 +210,10 @@
     wave_count = wave_local * ky_groups
     height = -(-(y_tile + 2) // 8) * 8
     chunk = 4 * 2 * wave_local * 3 * level_count // lanes
-    table_hi, table_lo = x_tables(kx_count, x_tile * ky_groups, x_tile)
+    table_x = x_tables(kx_count)
     table_y = y_tables(wave_count, y_tile * gz_groups, y_tile, wave_local, height)
     vmem = pl.BlockSpec(memory_space=pltpu.VMEM)
+    anywhere = pl.BlockSpec(memory_space=pl.ANY)
 
     def x_call(*refs):
         x_kernel(ky_groups, level_count, wave_count, *refs)
@@ -192,34 +221,37 @@
     def y_call(*refs):
         y_kernel(ky_groups, wave_local, height, *refs)
 
+    comp = jnp.transpose(complementary, (0, 2, 1, 3)).reshape(x_tile, 3 * level_count, y_tile)
     with jax.named_scope("x_transform"):
         sent = pl.pallas_call(
             x_call,
             out_shape=jax.ShapeDtypeStruct((ky_groups * chunk, lanes), f32),
-            in_specs=[vmem] * 3,
+            in_specs=[anywhere] * 2,
             out_specs=vmem,
-            compiler_params=pltpu.CompilerParams(vmem_limit_bytes=48 * 2**20),
+            scratch_shapes=[
+                pltpu.VMEM(amplitudes.shape, f32),
+                pltpu.VMEM(table_x.shape, f32),
+                pltpu.SemaphoreType.DMA((2,)),
+            ],
             name="x_transform",
-        )(amplitudes, jnp.asarray(table_hi), jnp.asarray(table_lo))
-    comp = jnp.transpose(complementary, (0, 2, 1, 3))
-    halos = []
-    for axis, size in (("ky", ky_groups), ("gz", gz_groups)):
-        up = [(i, i + 1) for i in range(size - 1)]
-        halos.append(lax.ppermute(comp, axis, up))
-        halos.append(lax.ppermute(comp, axis, [(j, i) for i, j in up]))
-    received = lax.all_to_all(sent.reshape(ky_groups, chunk, lanes), "ky", 0, 0)
+        )(amplitudes, jnp.asarray(table_x))
+    halos = [
+        lax.ppermute(comp, axis, swaps(lax.axis_size(axis), first)) for axis, first in ORDER
+    ]
+    x_in, x_out, y_in, y_out = (halos[ORDER.index(which)] for which in PAIRS)
+    received = lax.all_to_all(sent.reshape(ky_groups, 1, chunk * lanes), "ky", 0, 0)
     table = lax.dynamic_index_in_dim(jnp.asarray(table_y), lax.axis_index("gz"), 0, keepdims=False)
-    result = jax.ShapeDtypeStruct(comp.shape, f32)
+    result = jax.ShapeDtypeStruct((x_tile, 3, level_count, y_tile), f32)
     with jax.named_scope("y_transform_and_step"):
         incident, predicted = pl.pallas_call(
             y_call,
             out_shape=(result, result),
             in_specs=[vmem] * 7,
             out_specs=(vmem, vmem),
-            scratch_shapes=[pltpu.VMEM((4, 3, level_count, lanes), f32)],
+            scratch_shapes=[pltpu.VMEM((4, 3 * level_count, lanes), f32)],
             compiler_params=pltpu.CompilerParams(vmem_limit_bytes=48 * 2**20),
             name="y_transform",
-        )(received.reshape(ky_groups * chunk, lanes), table, comp, *halos)
+        )(received.reshape(ky_groups * chunk, lanes), table, comp, y_out, y_in, x_out, x_in)
     back = (0, 2, 1, 3)
     return jnp.transpose(incident, back), jnp.transpose(predicted, back)
 

time: 46.5 us -> 36.9 us (0.79)
  the two profiles are of different devices: /device:TPU:14 before, /device:TPU:59 now
where the time goes in v2:
time: 36.9 us; the launch traced here: 36.6 us
  starting transfers between devices  30.1 us (82%)
  Pallas kernels  4.9 us (13%)
  local copies, waits for them, and re-layouts  0.94 us (3%)
  between operations  0.74 us (2%)
    ppermute x4, starting transfers between devices, on_device(): lax.ppermute(comp, axis, swaps(lax.axis_size(axis), first))  15.4 us
    all_to_all x1, starting transfers between devices, on_device(): lax.all_to_all(sent.reshape(ky_groups, 1, chunk * lanes), 'ky', 0, 0)  14.7 us
    pallas_call x1, Pallas kernels, on_device(): pl.pallas_call(x_call, out_shape=jax.ShapeDtypeStruct((ky_groups * chunk,...  3.15 us
    pallas_call x1, Pallas kernels, on_device(): pl.pallas_call(y_call, out_shape=(result, result), in_specs=[vmem] * 7, o...  1.75 us
    squeeze x1, local copies, waits for them, and re-layouts, on_device(): lax.dynamic_index_in_dim(jnp.asarray(table_y), lax.axis_index('gz'), 0, k...  0.93 us
  transfers between devices with their start and end apart: 5, of which 0 were waited for; matrix products, arithmetic and copies ran while one was open for 3% of the time, Pallas kernels for 0%

profile of v2, /device:TPU:59, one launch (start us, length us, event | category | flops | bytes accessed | tf_op | source)
XLA Modules:
  0.0 36.6 jit_solution(2819068650032289170)
XLA Ops:
  0.6 0.0 copy-start
  0.6 3.2 %x_transform.1 = f32[768,128]{1,0:T(8,128)} custom-call(f32[2,8,1024]{2,1,0:T(8,128)} %refs_0_.1, f32[2,24,1024]{2,1,0:T(8,128)} %constant.14.clone.refs_1_), custom_call_target="tpu_custom_call" | custom-call | tf_op jit(solution)/shard_map/x_transform/x_transform/pallas_call | solution.py:226
  3.8 14.7 %all-to-all-start = ((f32[64,1,1536]{2,1,0:T(1,128)}), f32[64,1,1536]{2,1,0:T(1,128)S(1)}, u32[]{:S(2)}, u32[]{:S(2)}) async-start(f32[64,1,1536]{2,1,0:T(1,128)} %bitcast.15), calls=%async_computation | async-start | bytes 786432 | tf_op jit(solution)/shard_map/all_to_all | solution.py:242
  18.5 0.0 copy-done
  18.5 3.1 %collective-permute-start = (f32[2,24,32]{2,1,0:T(8,128)S(1)}, f32[2,24,32]{2,1,0:T(8,128)S(1)}, u32[]{:S(2)}, u32[]{:S(2)}) collective-permute-start(f32[2,24,32]{2,1,0:T(8,128)S(1)} %bitcast.10), channel_id=1, source_target_pairs={{1,2},{3,4},{5,6},{2,1},{4,3},{6,5},{9,10},{11,12},{13,14},{10,9},... | collective-permute-start | bytes 18440 | tf_op jit(solution)/shard_map/ppermute | solution.py:239
  21.6 5.7 %collective-permute-start.1 = (f32[2,24,32]{2,1,0:T(8,128)S(1)}, f32[2,24,32]{2,1,0:T(8,128)S(1)}, u32[]{:S(2)}, u32[]{:S(2)}) collective-permute-start(f32[2,24,32]{2,1,0:T(8,128)S(1)} %bitcast.11), channel_id=1, source_target_pairs={{0,1},{2,3},{4,5},{6,7},{1,0},{3,2},{5,4},{7,6},{8,9},{10,11},{12,... | collective-permute-start | bytes 18440 | tf_op jit(solution)/shard_map/ppermute | solution.py:239
  27.3 3.9 %collective-permute-start.2 = (f32[2,24,32]{2,1,0:T(8,128)S(1)}, f32[2,24,32]{2,1,0:T(8,128)S(1)}, u32[]{:S(2)}, u32[]{:S(2)}) collective-permute-start(f32[2,24,32]{2,1,0:T(8,128)S(1)} %bitcast.12), channel_id=1, source_target_pairs={{8,16},{24,32},{40,48},{56,64},{72,80},{88,96},{104,112},{120,128}... | collective-permute-start | bytes 18440 | tf_op jit(solution)/shard_map/ppermute | solution.py:239
  31.2 2.7 %collective-permute-start.3 = (f32[2,24,32]{2,1,0:T(8,128)S(1)}, f32[2,24,32]{2,1,0:T(8,128)S(1)}, u32[]{:S(2)}, u32[]{:S(2)}) collective-permute-start(f32[2,24,32]{2,1,0:T(8,128)S(1)} %bitcast.13), channel_id=1, source_target_pairs={{0,8},{16,24},{32,40},{48,56},{64,72},{80,88},{96,104},{112,120},{... | collective-permute-start | bytes 18440 | tf_op jit(solution)/shard_map/ppermute | solution.py:239
  33.9 0.9 %dynamic-slice_bitcast_fusion.refs_1_ = bf16[80,1024]{1,0:T(8,128)(2,1)S(1)} fusion(bf16[8,80,1024]{2,1,0:T(8,128)(2,1)} %constant.15.clone, s32[]{:T(128)S(6)} %select_n.4), kind=kLoop, calls=%fused_computation | loop fusion | bytes 327684 | tf_op jit(solution)/shard_map/jit(dynamic_index_in_dim)/squeeze | solution.py:243
  34.8 0.0 collective-permute-done.refs_3_
  34.8 0.0 collective-permute-done.1.refs_4_
  34.9 0.0 collective-permute-done.2.refs_5_
  34.9 0.0 collective-permute-done.3.refs_6_
  34.9 0.0 all-to-all-done
  34.9 1.7 %y_transform.1 = (f32[2,3,8,32]{3,2,1,0:T(8,128)}, f32[2,3,8,32]{3,2,1,0:T(8,128)}) custom-call(f32[768,128]{1,0:T(8,128)S(1)} %bitcast.9, bf16[80,1024]{1,0:T(8,128)(2,1)S(1)} %dynamic-slice_bitcast_fusion.refs_1_, f32[2,24,32]{2,1,0:T(8,128)S(1)} %bitcast.14, f32[2,24,32]{2,1,0:T(8,128)S(1)} %collective-permute-done.refs_3_, ...), custom_call_target="tpu_custom_call" | custom-call | tf_op jit(solution)/shard_map/y_transform_and_step/y_transform/pallas_call | solution.py:246
Async XLA Ops:
  0.6 17.8 %copy-start = (f32[2,8,3,32]{3,1,2,0:T(8,128)S(1)}, f32[2,8,3,32]{3,1,2,0:T(8,128)}, u32[]{:S(2)}) copy-start(f32[2,8,3,32]{3,1,2,0:T(8,128)} %param.5) | copy-start | bytes 18436
  3.8 31.1 %all-to-all-start = ((f32[64,1,1536]{2,1,0:T(1,128)}), f32[64,1,1536]{2,1,0:T(1,128)S(1)}, u32[]{:S(2)}, u32[]{:S(2)}) async-start(f32[64,1,1536]{2,1,0:T(1,128)} %bitcast.15), calls=%async_computation | async-start | bytes 786432 | tf_op jit(solution)/shard_map/all_to_all | solution.py:242
  18.5 16.4 %collective-permute-start = (f32[2,24,32]{2,1,0:T(8,128)S(1)}, f32[2,24,32]{2,1,0:T(8,128)S(1)}, u32[]{:S(2)}, u32[]{:S(2)}) collective-permute-start(f32[2,24,32]{2,1,0:T(8,128)S(1)} %bitcast.10), channel_id=1, source_target_pairs={{1,2},{3,4},{5,6},{2,1},{4,3},{6,5},{9,10},{11,12},{13,14},{10,9},... | collective-permute-start | bytes 18440 | tf_op jit(solution)/shard_map/ppermute | solution.py:239
  21.6 13.2 %collective-permute-start.1 = (f32[2,24,32]{2,1,0:T(8,128)S(1)}, f32[2,24,32]{2,1,0:T(8,128)S(1)}, u32[]{:S(2)}, u32[]{:S(2)}) collective-permute-start(f32[2,24,32]{2,1,0:T(8,128)S(1)} %bitcast.11), channel_id=1, source_target_pairs={{0,1},{2,3},{4,5},{6,7},{1,0},{3,2},{5,4},{7,6},{8,9},{10,11},{12,... | collective-permute-start | bytes 18440 | tf_op jit(solution)/shard_map/ppermute | solution.py:239
  27.3 7.6 %collective-permute-start.2 = (f32[2,24,32]{2,1,0:T(8,128)S(1)}, f32[2,24,32]{2,1,0:T(8,128)S(1)}, u32[]{:S(2)}, u32[]{:S(2)}) collective-permute-start(f32[2,24,32]{2,1,0:T(8,128)S(1)} %bitcast.12), channel_id=1, source_target_pairs={{8,16},{24,32},{40,48},{56,64},{72,80},{88,96},{104,112},{120,128}... | collective-permute-start | bytes 18440 | tf_op jit(solution)/shard_map/ppermute | solution.py:239
  31.2 3.7 %collective-permute-start.3 = (f32[2,24,32]{2,1,0:T(8,128)S(1)}, f32[2,24,32]{2,1,0:T(8,128)S(1)}, u32[]{:S(2)}, u32[]{:S(2)}) collective-permute-start(f32[2,24,32]{2,1,0:T(8,128)S(1)} %bitcast.13), channel_id=1, source_target_pairs={{0,8},{16,24},{32,40},{48,56},{64,72},{80,88},{96,104},{112,120},{... | collective-permute-start | bytes 18440 | tf_op jit(solution)/shard_map/ppermute | solution.py:239

commit v3 on v2

--- a/solution.py
+++ b/solution.py
@@ -1,6 +1,5 @@
 import jax
 import jax.numpy as jnp
-import ml_dtypes
 import numpy as np
 from jax import lax
 from jax.experimental import pallas as pl
@@ -20,42 +19,59 @@
     return high, (x - high.astype(f32)).astype(jnp.bfloat16)
 
 
-def split_table(table):
-    high = table.astype(np.float32).astype(ml_dtypes.bfloat16)
-    return high, (table - high.astype(np.float64)).astype(np.float32).astype(ml_dtypes.bfloat16)
-
-
-def x_tables(kx_count):
-    near = np.arange(16).reshape(8, 2).T.reshape(-1) * 2 + 1
-    halves = np.concatenate([near, 32 * np.arange(8)])
-    turns = np.outer(halves, np.arange(kx_count)) % int(2 * band_factor * kx_count)
-    phase = turns * (2.0 * np.pi / (2 * band_factor * kx_count))
-    return np.stack([np.cos(phase), np.sin(phase)]).astype(np.float32)
-
-
-def y_tables(wave_count, zone_y, y_tile, wave_local, height):
-    tiles = zone_y // y_tile
-    cells = np.arange(tiles)[:, None] * y_tile + np.arange(y_tile + 2)[None] - 1
-    inside = (cells >= 0) & (cells < zone_y)
-    rows = np.arange(wave_count).reshape(-1, wave_local).T.reshape(-1) - wave_count // 2
-    turns = (cells[..., None] * 2 + 1) * rows % int(2 * band_factor * wave_count)
-    phase = turns * (2.0 * np.pi / (2 * band_factor * wave_count))
-    table = np.concatenate([np.cos(phase), -np.sin(phase)], axis=-1) * inside[..., None]
-    table = np.pad(table, ((0, 0), (0, height - table.shape[1]), (0, 0)))
-    return np.concatenate(split_table(table), axis=1)
+def cos_sin(turns, period):
+    quarter = period // 4
+    turns = turns & (period - 1)
+    which = ((turns + quarter // 2) // quarter) & 3
+    angle = (turns - (turns + quarter // 2) // quarter * quarter).astype(f32) * (2.0 * np.pi / period)
+    square = angle * angle
+    sin, cos = jnp.full_like(square, 1.0), jnp.full_like(square, 1.0)
+    for n in (8, 6, 4, 2):
+        sin = 1.0 - sin * square * (1.0 / (n * (n + 1)))
+    for n in (9, 7, 5, 3, 1):
+        cos = 1.0 - cos * square * (1.0 / (n * (n + 1)))
+    sin = sin * angle
+    swapped = (which & 1) == 1
+    first, second = jnp.where(swapped, sin, cos), jnp.where(swapped, cos, sin)
+    return (
+        jnp.where((which == 1) | (which == 2), -first, first),
+        jnp.where(which >= 2, -second, second),
+    )
+
+
+def x_tables(ky_groups, kx_count):
+    period = int(2 * band_factor * kx_count)
+    row = lax.broadcasted_iota(jnp.int32, (24, kx_count), 0)
+    halves = jnp.where(row < 16, row % 8 * 4 + row // 8 * 2 + 1, 32 * (row - 16))
+    cos, sin = cos_sin(halves * lax.broadcasted_iota(jnp.int32, (24, kx_count), 1), period)
+    cos_rows, sin_rows = [], []
+    for e in range(2):
+        near = slice(8 * e, 8 * e + 8)
+        for i in range(ky_groups // 8):
+            far = slice(16 + i, 17 + i)
+            cos_rows.append(cos[near] * cos[far] - sin[near] * sin[far])
+            sin_rows.append(sin[near] * cos[far] + cos[near] * sin[far])
+    return jnp.concatenate(cos_rows + sin_rows, axis=0)
+
+
+def y_tables(y_tile, ky_groups, wave_local, height):
+    wave_count = ky_groups * wave_local
+    shape = (height, wave_count)
+    row, column = (lax.broadcasted_iota(jnp.int32, shape, axis) for axis in (0, 1))
+    cell = lax.axis_index("gz") * y_tile + row - 1
+    inside = (cell >= 0) & (cell < lax.axis_size("gz") * y_tile) & (row < y_tile + 2)
+    wave = column % ky_groups * wave_local + column // ky_groups - wave_count // 2
+    cos, sin = cos_sin((2 * cell + 1) * wave, int(2 * band_factor * wave_count))
+    return jnp.concatenate([jnp.where(inside, cos, 0.0), jnp.where(inside, -sin, 0.0)], axis=1)
 
 
 def dot_nt(a, b):
     return lax.dot_general(a, b, (((1,), (1,)), ((), ())), preferred_element_type=f32)
 
 
-def x_kernel(ky_groups, level_count, wave_count, amplitudes, tables, out, modes, table, sems):
-    copies = [
-        pltpu.make_async_copy(source, target, sems.at[i])
-        for i, (source, target) in enumerate(((tables, table), (amplitudes, modes)))
-    ]
-    for copy in copies:
-        copy.start()
+def x_kernel(ky_groups, level_count, wave_count, amplitudes, out, modes, sem):
+    copy = pltpu.make_async_copy(amplitudes, modes, sem)
+    copy.start()
     wave_local, kx_count = amplitudes.shape[1:]
     per_row = 3 * level_count
     me = lax.axis_index("ky")
@@ -70,16 +86,8 @@
     depths = -(lax.broadcasted_iota(jnp.int32, shape, 0).astype(f32) + 0.5) * cell_height
     kx = along_x[0:1]
     decays = [jnp.exp(jnp.broadcast_to(magnitude[n : n + 1], shape) * depths) for n in range(wave_local)]
-    copies[0].wait()
-    cos_rows, sin_rows = [], []
-    for e in range(2):
-        cos_near, sin_near = table[0, 8 * e : 8 * e + 8], table[1, 8 * e : 8 * e + 8]
-        for i in range(ky_groups // 8):
-            cos_far, sin_far = table[0, 16 + i : 17 + i], table[1, 16 + i : 17 + i]
-            cos_rows.append(cos_near * cos_far - sin_near * sin_far)
-            sin_rows.append(sin_near * cos_far + cos_near * sin_far)
-    table_hi, table_lo = split(jnp.concatenate(cos_rows + sin_rows, axis=0))
-    copies[1].wait()
+    table_hi, table_lo = split(x_tables(ky_groups, kx_count))
+    copy.wait()
     parts_re, parts_im = [], []
     for n in range(wave_local):
         k = magnitude[n : n + 1]
@@ -118,7 +126,7 @@
     return [total * comp[c] + comp[normal] * inc[c] for c in range(3)]
 
 
-def y_kernel(ky_groups, wave_local, height, received, table, comp, y_out, y_in, x_out, x_in, incident, predicted, padded):
+def y_kernel(ky_groups, wave_local, height, received, comp, y_out, y_in, x_out, x_in, incident, predicted, padded):
     per_row, y_tile = comp.shape[1:]
     level_count = per_row // 3
     width = 2 * wave_local * per_row // lanes
@@ -139,9 +147,10 @@
             block = piece if block is None else jnp.where(lane < at, block, piece)
         blocks.append(block)
     modes_hi, modes_lo = split(jnp.concatenate(blocks, axis=0))
-    both = jnp.dot(table[...], modes_hi, preferred_element_type=f32)
+    table_hi, table_lo = split(y_tables(y_tile, ky_groups, wave_local, height))
+    both = jnp.dot(jnp.concatenate([table_hi, table_lo], axis=0), modes_hi, preferred_element_type=f32)
     field = both[:height] + both[height:]
-    field += jnp.dot(table[:height], modes_lo, preferred_element_type=f32)
+    field += jnp.dot(table_hi, modes_lo, preferred_element_type=f32)
     field = jnp.concatenate([field, jnp.zeros((lanes - height, lanes), f32)], axis=0).T
     inc = [
         [field[(k * 3 + c) * level_count : (k * 3 + c + 1) * level_count] for c in range(3)]
@@ -208,10 +217,8 @@
     ky_groups, gz_groups = lax.axis_size("ky"), lax.axis_size("gz")
     wave_local, kx_count = amplitudes.shape[1:]
     wave_count = wave_local * ky_groups
-    height = -(-(y_tile + 2) // 8) * 8
+    height = -(-(y_tile + 2) // 16) * 16
     chunk = 4 * 2 * wave_local * 3 * level_count // lanes
-    table_x = x_tables(kx_count)
-    table_y = y_tables(wave_count, y_tile * gz_groups, y_tile, wave_local, height)
     vmem = pl.BlockSpec(memory_space=pltpu.VMEM)
     anywhere = pl.BlockSpec(memory_space=pl.ANY)
 
@@ -226,32 +233,30 @@
         sent = pl.pallas_call(
             x_call,
             out_shape=jax.ShapeDtypeStruct((ky_groups * chunk, lanes), f32),
-            in_specs=[anywhere] * 2,
+            in_specs=[anywhere],
             out_specs=vmem,
             scratch_shapes=[
                 pltpu.VMEM(amplitudes.shape, f32),
-                pltpu.VMEM(table_x.shape, f32),
-                pltpu.SemaphoreType.DMA((2,)),
+                pltpu.SemaphoreType.DMA,
             ],
             name="x_transform",
-        )(amplitudes, jnp.asarray(table_x))
+        )(amplitudes)
     halos = [
         lax.ppermute(comp, axis, swaps(lax.axis_size(axis), first)) for axis, first in ORDER
     ]
     x_in, x_out, y_in, y_out = (halos[ORDER.index(which)] for which in PAIRS)
     received = lax.all_to_all(sent.reshape(ky_groups, 1, chunk * lanes), "ky", 0, 0)
-    table = lax.dynamic_index_in_dim(jnp.asarray(table_y), lax.axis_index("gz"), 0, keepdims=False)
     result = jax.ShapeDtypeStruct((x_tile, 3, level_count, y_tile), f32)
     with jax.named_scope("y_transform_and_step"):
         incident, predicted = pl.pallas_call(
             y_call,
             out_shape=(result, result),
-            in_specs=[vmem] * 7,
+            in_specs=[vmem] * 6,
             out_specs=(vmem, vmem),
             scratch_shapes=[pltpu.VMEM((4, 3 * level_count, lanes), f32)],
             compiler_params=pltpu.CompilerParams(vmem_limit_bytes=48 * 2**20),
             name="y_transform",
-        )(received.reshape(ky_groups * chunk, lanes), table, comp, y_out, y_in, x_out, x_in)
+        )(received.reshape(ky_groups * chunk, lanes), comp, y_out, y_in, x_out, x_in)
     back = (0, 2, 1, 3)
     return jnp.transpose(incident, back), jnp.transpose(predicted, back)
 

time: 36.9 us -> 36.5 us (0.989)
  the two profiles are of different devices: /device:TPU:59 before, /device:TPU:58 now
where the time goes in v3:
time: 36.5 us; the launch traced here: 36.1 us
  starting transfers between devices  29.4 us (81%)
  Pallas kernels  4.5 us (12%)
  waiting for transfers between devices  1.55 us (4%)
  between operations  0.71 us (2%)
    ppermute x4, starting transfers between devices, on_device(): lax.ppermute(comp, axis, swaps(lax.axis_size(axis), first))  15 us
    all_to_all x1, starting transfers between devices, on_device(): lax.all_to_all(sent.reshape(ky_groups, 1, chunk * lanes), 'ky', 0, 0)  14.3 us
    pallas_call x1, Pallas kernels, on_device(): pl.pallas_call(x_call, out_shape=jax.ShapeDtypeStruct((ky_groups * chunk,...  2.71 us
    pallas_call x1, Pallas kernels, on_device(): pl.pallas_call(y_call, out_shape=(result, result), in_specs=[vmem] * 6, o...  1.78 us
    ppermute x4, waiting for transfers between devices, on_device(): lax.ppermute(comp, axis, swaps(lax.axis_size(axis), first))  1.54 us
  transfers between devices with their start and end apart: 5, of which 1 were waited for; matrix products, arithmetic and copies ran while one was open for 0% of the time, Pallas kernels for 0%

profile of v3, /device:TPU:58, one launch (start us, length us, event | category | flops | bytes accessed | tf_op | source)
XLA Modules:
  0.0 36.1 jit_solution(10384491488744619772)
XLA Ops:
  0.6 2.7 %x_transform.1 = f32[768,128]{1,0:T(8,128)} custom-call(f32[2,8,1024]{2,1,0:T(8,128)} %refs_0_.1), custom_call_target="tpu_custom_call" | custom-call | tf_op jit(solution)/shard_map/x_transform/x_transform/pallas_call | solution.py:233
  3.4 0.0 copy-start
  3.4 14.3 %all-to-all-start = ((f32[64,1,1536]{2,1,0:T(1,128)}), f32[64,1,1536]{2,1,0:T(1,128)S(1)}, u32[]{:S(2)}, u32[]{:S(2)}) async-start(f32[64,1,1536]{2,1,0:T(1,128)} %bitcast.13), calls=%async_computation | async-start | bytes 786432 | tf_op jit(solution)/shard_map/all_to_all | solution.py:248
  17.7 0.0 copy-done
  17.7 3.4 %collective-permute-start = (f32[2,24,32]{2,1,0:T(8,128)S(1)}, f32[2,24,32]{2,1,0:T(8,128)S(1)}, u32[]{:S(2)}, u32[]{:S(2)}) collective-permute-start(f32[2,24,32]{2,1,0:T(8,128)S(1)} %bitcast.8), channel_id=1, source_target_pairs={{1,2},{3,4},{5,6},{2,1},{4,3},{6,5},{9,10},{11,12},{13,14},{10,9},... | collective-permute-start | bytes 18440 | tf_op jit(solution)/shard_map/ppermute | solution.py:245
  21.1 6.0 %collective-permute-start.1 = (f32[2,24,32]{2,1,0:T(8,128)S(1)}, f32[2,24,32]{2,1,0:T(8,128)S(1)}, u32[]{:S(2)}, u32[]{:S(2)}) collective-permute-start(f32[2,24,32]{2,1,0:T(8,128)S(1)} %bitcast.9), channel_id=1, source_target_pairs={{0,1},{2,3},{4,5},{6,7},{1,0},{3,2},{5,4},{7,6},{8,9},{10,11},{12,... | collective-permute-start | bytes 18440 | tf_op jit(solution)/shard_map/ppermute | solution.py:245
  27.1 3.8 %collective-permute-start.2 = (f32[2,24,32]{2,1,0:T(8,128)S(1)}, f32[2,24,32]{2,1,0:T(8,128)S(1)}, u32[]{:S(2)}, u32[]{:S(2)}) collective-permute-start(f32[2,24,32]{2,1,0:T(8,128)S(1)} %bitcast.10), channel_id=1, source_target_pairs={{8,16},{24,32},{40,48},{56,64},{72,80},{88,96},{104,112},{120,128}... | collective-permute-start | bytes 18440 | tf_op jit(solution)/shard_map/ppermute | solution.py:245
  30.9 1.9 %collective-permute-start.3 = (f32[2,24,32]{2,1,0:T(8,128)S(1)}, f32[2,24,32]{2,1,0:T(8,128)S(1)}, u32[]{:S(2)}, u32[]{:S(2)}) collective-permute-start(f32[2,24,32]{2,1,0:T(8,128)S(1)} %bitcast.11), channel_id=1, source_target_pairs={{0,8},{16,24},{32,40},{48,56},{64,72},{80,88},{96,104},{112,120},{... | collective-permute-start | bytes 18440 | tf_op jit(solution)/shard_map/ppermute | solution.py:245
  32.8 0.0 collective-permute-done.refs_2_
  32.8 0.0 collective-permute-done.1.refs_3_
  32.8 1.5 %collective-permute-done.2.refs_4_ = f32[2,24,32]{2,1,0:T(8,128)S(1)} collective-permute-done((f32[2,24,32]{2,1,0:T(8,128)S(1)}, f32[2,24,32]{2,1,0:T(8,128)S(1)}, u32[]{:S(2)}, u32[]{:S(2)}) %collective-permute-start.2) | collective-permute-done | bytes 6176 | tf_op jit(solution)/shard_map/ppermute | solution.py:245
  34.4 0.0 collective-permute-done.3.refs_5_
  34.4 0.0 all-to-all-done
  34.4 1.8 %y_transform.1 = (f32[2,3,8,32]{3,2,1,0:T(8,128)}, f32[2,3,8,32]{3,2,1,0:T(8,128)}) custom-call(f32[768,128]{1,0:T(8,128)S(1)} %bitcast.7, f32[2,24,32]{2,1,0:T(8,128)S(1)} %bitcast.12, f32[2,24,32]{2,1,0:T(8,128)S(1)} %collective-permute-done.refs_2_, f32[2,24,32]{2,1,0:T(8,128)S(1)} %collective-permute-done.1.refs_3_, ...), custom_call_target="tpu_custom_call" | custom-call | tf_op jit(solution)/shard_map/y_transform_and_step/y_transform/pallas_call | solution.py:251
Async XLA Ops:
  3.4 14.4 %copy-start = (f32[2,8,3,32]{3,1,2,0:T(8,128)S(1)}, f32[2,8,3,32]{3,1,2,0:T(8,128)}, u32[]{:S(2)}) copy-start(f32[2,8,3,32]{3,1,2,0:T(8,128)} %param.3) | copy-start | bytes 18436
  3.4 31.0 %all-to-all-start = ((f32[64,1,1536]{2,1,0:T(1,128)}), f32[64,1,1536]{2,1,0:T(1,128)S(1)}, u32[]{:S(2)}, u32[]{:S(2)}) async-start(f32[64,1,1536]{2,1,0:T(1,128)} %bitcast.13), calls=%async_computation | async-start | bytes 786432 | tf_op jit(solution)/shard_map/all_to_all | solution.py:248
  17.7 15.1 %collective-permute-start = (f32[2,24,32]{2,1,0:T(8,128)S(1)}, f32[2,24,32]{2,1,0:T(8,128)S(1)}, u32[]{:S(2)}, u32[]{:S(2)}) collective-permute-start(f32[2,24,32]{2,1,0:T(8,128)S(1)} %bitcast.8), channel_id=1, source_target_pairs={{1,2},{3,4},{5,6},{2,1},{4,3},{6,5},{9,10},{11,12},{13,14},{10,9},... | collective-permute-start | bytes 18440 | tf_op jit(solution)/shard_map/ppermute | solution.py:245
  21.1 11.7 %collective-permute-start.1 = (f32[2,24,32]{2,1,0:T(8,128)S(1)}, f32[2,24,32]{2,1,0:T(8,128)S(1)}, u32[]{:S(2)}, u32[]{:S(2)}) collective-permute-start(f32[2,24,32]{2,1,0:T(8,128)S(1)} %bitcast.9), channel_id=1, source_target_pairs={{0,1},{2,3},{4,5},{6,7},{1,0},{3,2},{5,4},{7,6},{8,9},{10,11},{12,... | collective-permute-start | bytes 18440 | tf_op jit(solution)/shard_map/ppermute | solution.py:245
  27.1 7.3 %collective-permute-start.2 = (f32[2,24,32]{2,1,0:T(8,128)S(1)}, f32[2,24,32]{2,1,0:T(8,128)S(1)}, u32[]{:S(2)}, u32[]{:S(2)}) collective-permute-start(f32[2,24,32]{2,1,0:T(8,128)S(1)} %bitcast.10), channel_id=1, source_target_pairs={{8,16},{24,32},{40,48},{56,64},{72,80},{88,96},{104,112},{120,128}... | collective-permute-start | bytes 18440 | tf_op jit(solution)/shard_map/ppermute | solution.py:245
  30.9 3.5 %collective-permute-start.3 = (f32[2,24,32]{2,1,0:T(8,128)S(1)}, f32[2,24,32]{2,1,0:T(8,128)S(1)}, u32[]{:S(2)}, u32[]{:S(2)}) collective-permute-start(f32[2,24,32]{2,1,0:T(8,128)S(1)} %bitcast.11), channel_id=1, source_target_pairs={{0,8},{16,24},{32,40},{48,56},{64,72},{80,88},{96,104},{112,120},{... | collective-permute-start | bytes 18440 | tf_op jit(solution)/shard_map/ppermute | solution.py:245

commit v4 on v3

--- a/solution.py
+++ b/solution.py
@@ -39,19 +39,20 @@
     )
 
 
-def x_tables(ky_groups, kx_count):
+def x_tables(ky_groups, kx_count, centre):
     period = int(2 * band_factor * kx_count)
-    row = lax.broadcasted_iota(jnp.int32, (24, kx_count), 0)
+    row = lax.broadcasted_iota(jnp.int32, (32, kx_count), 0)
     halves = jnp.where(row < 16, row % 8 * 4 + row // 8 * 2 + 1, 32 * (row - 16))
-    cos, sin = cos_sin(halves * lax.broadcasted_iota(jnp.int32, (24, kx_count), 1), period)
+    halves = jnp.where(row < 24, halves, 2 * centre)
+    cos, sin = cos_sin(halves * lax.broadcasted_iota(jnp.int32, (32, kx_count), 1), period)
     cos_rows, sin_rows = [], []
     for e in range(2):
         near = slice(8 * e, 8 * e + 8)
-        for i in range(ky_groups // 8):
+        for i in range(ky_groups // 16):
             far = slice(16 + i, 17 + i)
             cos_rows.append(cos[near] * cos[far] - sin[near] * sin[far])
             sin_rows.append(sin[near] * cos[far] + cos[near] * sin[far])
-    return jnp.concatenate(cos_rows + sin_rows, axis=0)
+    return jnp.concatenate(cos_rows + sin_rows, axis=0), cos[24:], sin[24:]
 
 
 def y_tables(y_tile, ky_groups, wave_local, height):
@@ -60,7 +61,9 @@
     row, column = (lax.broadcasted_iota(jnp.int32, shape, axis) for axis in (0, 1))
     cell = lax.axis_index("gz") * y_tile + row - 1
     inside = (cell >= 0) & (cell < lax.axis_size("gz") * y_tile) & (row < y_tile + 2)
-    wave = column % ky_groups * wave_local + column // ky_groups - wave_count // 2
+    source = column % ky_groups
+    source = jnp.where(source < ky_groups // 2, ky_groups // 2 - 1 - source, source)
+    wave = source * wave_local + column // ky_groups - wave_count // 2
     cos, sin = cos_sin((2 * cell + 1) * wave, int(2 * band_factor * wave_count))
     return jnp.concatenate([jnp.where(inside, cos, 0.0), jnp.where(inside, -sin, 0.0)], axis=1)
 
@@ -86,14 +89,17 @@
     depths = -(lax.broadcasted_iota(jnp.int32, shape, 0).astype(f32) + 0.5) * cell_height
     kx = along_x[0:1]
     decays = [jnp.exp(jnp.broadcast_to(magnitude[n : n + 1], shape) * depths) for n in range(wave_local)]
-    table_hi, table_lo = split(x_tables(ky_groups, kx_count))
+    table, cos_centre, sin_centre = x_tables(ky_groups, kx_count, ky_groups)
+    table_hi, table_lo = split(table)
     copy.wait()
+    all_re = modes[0] * cos_centre - modes[1] * sin_centre
+    all_im = modes[0] * sin_centre + modes[1] * cos_centre
     parts_re, parts_im = [], []
     for n in range(wave_local):
         k = magnitude[n : n + 1]
         ky = along_y[n : n + 1]
-        re = decays[n] * modes[0, n : n + 1]
-        im = decays[n] * modes[1, n : n + 1]
+        re = decays[n] * all_re[n : n + 1]
+        im = decays[n] * all_im[n : n + 1]
         parts_re += [-kx * im, -ky * im, k * re]
         parts_im += [kx * re, ky * re, k * im]
     modes_hi, modes_lo = split(jnp.concatenate(parts_re + parts_im, axis=0))
@@ -103,18 +109,27 @@
     by_cos, by_sin = product[:half], product[half:]
     middle = wave_local * per_row
     turned = jnp.concatenate([-by_sin[:, middle:], by_sin[:, :middle]], axis=1)
-    field = by_cos + turned
-    even, odd = field[:ky_groups], field[ky_groups:]
-    width = field.shape[1] // lanes
+    upper, lower = by_cos + turned, by_cos - turned
+    count = ky_groups // 2
+    upper_first, upper_second = upper[:count], upper[count:]
+    lower_second, lower_first = lower[:count], lower[count:]
+    width = upper.shape[1] // lanes
     chunk = 4 * width
     for j in range(width):
         cut = slice(lanes * j, lanes * (j + 1))
-        out[pl.ds(j + chunk, ky_groups - 1, stride=chunk), :] = odd[: ky_groups - 1, cut]
-        out[pl.ds(j, 1), :] = jnp.zeros((1, lanes), f32)
-        out[pl.ds(j + width, ky_groups, stride=chunk), :] = even[:, cut]
-        out[pl.ds(j + 2 * width, ky_groups, stride=chunk), :] = odd[:, cut]
-        out[pl.ds(j + 3 * width, ky_groups - 1, stride=chunk), :] = even[1:, cut]
-        out[pl.ds((ky_groups - 1) * chunk + j + 3 * width, 1), :] = jnp.zeros((1, lanes), f32)
+        out[pl.ds(j, count - 1, stride=chunk), :] = lower_second[1:, cut]
+        out[pl.ds(j + (count - 1) * chunk, 1), :] = jnp.zeros((1, lanes), f32)
+        out[pl.ds(j + width, count, stride=chunk), :] = lower_first[:, cut]
+        out[pl.ds(j + 2 * width, count, stride=chunk), :] = lower_second[:, cut]
+        out[pl.ds(j + 3 * width, 1), :] = upper_first[:1, cut]
+        out[pl.ds(j + chunk + 3 * width, count - 1, stride=chunk), :] = lower_first[: count - 1, cut]
+        at = count * chunk + j
+        out[pl.ds(at, 1), :] = lower_second[:1, cut]
+        out[pl.ds(at + chunk, count - 1, stride=chunk), :] = upper_second[: count - 1, cut]
+        out[pl.ds(at + width, count, stride=chunk), :] = upper_first[:, cut]
+        out[pl.ds(at + 2 * width, count, stride=chunk), :] = upper_second[:, cut]
+        out[pl.ds(at + 3 * width, count - 1, stride=chunk), :] = upper_first[1:, cut]
+        out[pl.ds(at + (count - 1) * chunk + 3 * width, 1), :] = jnp.zeros((1, lanes), f32)
 
 
 def face(a, b):
@@ -245,7 +260,9 @@
         lax.ppermute(comp, axis, swaps(lax.axis_size(axis), first)) for axis, first in ORDER
     ]
     x_in, x_out, y_in, y_out = (halos[ORDER.index(which)] for which in PAIRS)
-    received = lax.all_to_all(sent.reshape(ky_groups, 1, chunk * lanes), "ky", 0, 0)
+    order = [*range(ky_groups // 2 - 1, -1, -1), *range(ky_groups // 2, ky_groups)]
+    sent = sent.reshape(ky_groups, 1, chunk * lanes)
+    received = lax.all_to_all(sent, "ky", 0, 0, axis_index_groups=[order])
     result = jax.ShapeDtypeStruct((x_tile, 3, level_count, y_tile), f32)
     with jax.named_scope("y_transform_and_step"):
         incident, predicted = pl.pallas_call(

time: 36.5 us -> 35.7 us (0.978)
  the two profiles are of different devices: /device:TPU:58 before, /device:TPU:5 now
where the time goes in v4:
time: 35.7 us; the launch traced here: 35.4 us
  starting transfers between devices  29.2 us (82%)
  Pallas kernels  4.31 us (12%)
  waiting for transfers between devices  1.14 us (3%)
  between operations  0.72 us (2%)
    ppermute x4, starting transfers between devices, on_device(): lax.ppermute(comp, axis, swaps(lax.axis_size(axis), first))  14.6 us
    all_to_all x1, starting transfers between devices, on_device(): received = lax.all_to_all(sent, 'ky', 0, 0, axis_index_groups=[order])  14.6 us
    pallas_call x1, Pallas kernels, on_device(): pl.pallas_call(x_call, out_shape=jax.ShapeDtypeStruct((ky_groups * chunk,...  2.53 us
    pallas_call x1, Pallas kernels, on_device(): pl.pallas_call(y_call, out_shape=(result, result), in_specs=[vmem] * 6, o...  1.78 us
    ppermute x4, waiting for transfers between devices, on_device(): lax.ppermute(comp, axis, swaps(lax.axis_size(axis), first))  1.14 us
  transfers between devices with their start and end apart: 5, of which 1 were waited for; matrix products, arithmetic and copies ran while one was open for 0% of the time, Pallas kernels for 0%

profile of v4, /device:TPU:5, one launch (start us, length us, event | category | flops | bytes accessed | tf_op | source)
XLA Modules:
  0.0 35.4 jit_solution(17393622983652547223)
XLA Ops:
  0.6 2.5 %x_transform.1 = f32[768,128]{1,0:T(8,128)} custom-call(f32[2,8,1024]{2,1,0:T(8,128)} %refs_0_.1), custom_call_target="tpu_custom_call" | custom-call | tf_op jit(solution)/shard_map/x_transform/x_transform/pallas_call | solution.py:248
  3.2 0.0 copy-start
  3.2 14.6 %all-to-all-start = ((f32[64,1,1536]{2,1,0:T(1,128)}), f32[64,1,1536]{2,1,0:T(1,128)S(1)}, u32[]{:S(2)}, u32[]{:S(2)}) async-start(f32[64,1,1536]{2,1,0:T(1,128)} %bitcast.13), calls=%async_computation | async-start | bytes 786432 | tf_op jit(solution)/shard_map/all_to_all | solution.py:265
  17.8 0.0 copy-done
  17.8 2.2 %collective-permute-start = (f32[2,24,32]{2,1,0:T(8,128)S(1)}, f32[2,24,32]{2,1,0:T(8,128)S(1)}, u32[]{:S(2)}, u32[]{:S(2)}) collective-permute-start(f32[2,24,32]{2,1,0:T(8,128)S(1)} %bitcast.8), channel_id=1, source_target_pairs={{1,2},{3,4},{5,6},{2,1},{4,3},{6,5},{9,10},{11,12},{13,14},{10,9},... | collective-permute-start | bytes 18440 | tf_op jit(solution)/shard_map/ppermute | solution.py:260
  19.9 6.6 %collective-permute-start.1 = (f32[2,24,32]{2,1,0:T(8,128)S(1)}, f32[2,24,32]{2,1,0:T(8,128)S(1)}, u32[]{:S(2)}, u32[]{:S(2)}) collective-permute-start(f32[2,24,32]{2,1,0:T(8,128)S(1)} %bitcast.9), channel_id=1, source_target_pairs={{0,1},{2,3},{4,5},{6,7},{1,0},{3,2},{5,4},{7,6},{8,9},{10,11},{12,... | collective-permute-start | bytes 18440 | tf_op jit(solution)/shard_map/ppermute | solution.py:260
  26.5 4.0 %collective-permute-start.2 = (f32[2,24,32]{2,1,0:T(8,128)S(1)}, f32[2,24,32]{2,1,0:T(8,128)S(1)}, u32[]{:S(2)}, u32[]{:S(2)}) collective-permute-start(f32[2,24,32]{2,1,0:T(8,128)S(1)} %bitcast.10), channel_id=1, source_target_pairs={{8,16},{24,32},{40,48},{56,64},{72,80},{88,96},{104,112},{120,128}... | collective-permute-start | bytes 18440 | tf_op jit(solution)/shard_map/ppermute | solution.py:260
  30.5 1.9 %collective-permute-start.3 = (f32[2,24,32]{2,1,0:T(8,128)S(1)}, f32[2,24,32]{2,1,0:T(8,128)S(1)}, u32[]{:S(2)}, u32[]{:S(2)}) collective-permute-start(f32[2,24,32]{2,1,0:T(8,128)S(1)} %bitcast.11), channel_id=1, source_target_pairs={{0,8},{16,24},{32,40},{48,56},{64,72},{80,88},{96,104},{112,120},{... | collective-permute-start | bytes 18440 | tf_op jit(solution)/shard_map/ppermute | solution.py:260
  32.4 0.0 collective-permute-done.refs_2_
  32.4 0.0 collective-permute-done.1.refs_3_
  32.5 0.0 collective-permute-done.2.refs_4_
  32.5 1.1 %collective-permute-done.3.refs_5_ = f32[2,24,32]{2,1,0:T(8,128)S(1)} collective-permute-done((f32[2,24,32]{2,1,0:T(8,128)S(1)}, f32[2,24,32]{2,1,0:T(8,128)S(1)}, u32[]{:S(2)}, u32[]{:S(2)}) %collective-permute-start.3) | collective-permute-done | bytes 6176 | tf_op jit(solution)/shard_map/ppermute | solution.py:260
  33.6 0.0 all-to-all-done
  33.6 1.8 %y_transform.1 = (f32[2,3,8,32]{3,2,1,0:T(8,128)}, f32[2,3,8,32]{3,2,1,0:T(8,128)}) custom-call(f32[768,128]{1,0:T(8,128)S(1)} %bitcast.7, f32[2,24,32]{2,1,0:T(8,128)S(1)} %bitcast.12, f32[2,24,32]{2,1,0:T(8,128)S(1)} %collective-permute-done.refs_2_, f32[2,24,32]{2,1,0:T(8,128)S(1)} %collective-permute-done.1.refs_3_, ...), custom_call_target="tpu_custom_call" | custom-call | tf_op jit(solution)/shard_map/y_transform_and_step/y_transform/pallas_call | solution.py:268
Async XLA Ops:
  3.2 14.6 %copy-start = (f32[2,8,3,32]{3,1,2,0:T(8,128)S(1)}, f32[2,8,3,32]{3,1,2,0:T(8,128)}, u32[]{:S(2)}) copy-start(f32[2,8,3,32]{3,1,2,0:T(8,128)} %param.3) | copy-start | bytes 18436
  3.2 30.4 %all-to-all-start = ((f32[64,1,1536]{2,1,0:T(1,128)}), f32[64,1,1536]{2,1,0:T(1,128)S(1)}, u32[]{:S(2)}, u32[]{:S(2)}) async-start(f32[64,1,1536]{2,1,0:T(1,128)} %bitcast.13), calls=%async_computation | async-start | bytes 786432 | tf_op jit(solution)/shard_map/all_to_all | solution.py:265
  17.8 14.7 %collective-permute-start = (f32[2,24,32]{2,1,0:T(8,128)S(1)}, f32[2,24,32]{2,1,0:T(8,128)S(1)}, u32[]{:S(2)}, u32[]{:S(2)}) collective-permute-start(f32[2,24,32]{2,1,0:T(8,128)S(1)} %bitcast.8), channel_id=1, source_target_pairs={{1,2},{3,4},{5,6},{2,1},{4,3},{6,5},{9,10},{11,12},{13,14},{10,9},... | collective-permute-start | bytes 18440 | tf_op jit(solution)/shard_map/ppermute | solution.py:260
  19.9 12.5 %collective-permute-start.1 = (f32[2,24,32]{2,1,0:T(8,128)S(1)}, f32[2,24,32]{2,1,0:T(8,128)S(1)}, u32[]{:S(2)}, u32[]{:S(2)}) collective-permute-start(f32[2,24,32]{2,1,0:T(8,128)S(1)} %bitcast.9), channel_id=1, source_target_pairs={{0,1},{2,3},{4,5},{6,7},{1,0},{3,2},{5,4},{7,6},{8,9},{10,11},{12,... | collective-permute-start | bytes 18440 | tf_op jit(solution)/shard_map/ppermute | solution.py:260
  26.5 5.9 %collective-permute-start.2 = (f32[2,24,32]{2,1,0:T(8,128)S(1)}, f32[2,24,32]{2,1,0:T(8,128)S(1)}, u32[]{:S(2)}, u32[]{:S(2)}) collective-permute-start(f32[2,24,32]{2,1,0:T(8,128)S(1)} %bitcast.10), channel_id=1, source_target_pairs={{8,16},{24,32},{40,48},{56,64},{72,80},{88,96},{104,112},{120,128}... | collective-permute-start | bytes 18440 | tf_op jit(solution)/shard_map/ppermute | solution.py:260
  30.5 3.1 %collective-permute-start.3 = (f32[2,24,32]{2,1,0:T(8,128)S(1)}, f32[2,24,32]{2,1,0:T(8,128)S(1)}, u32[]{:S(2)}, u32[]{:S(2)}) collective-permute-start(f32[2,24,32]{2,1,0:T(8,128)S(1)} %bitcast.11), channel_id=1, source_target_pairs={{0,8},{16,24},{32,40},{48,56},{64,72},{80,88},{96,104},{112,120},{... | collective-permute-start | bytes 18440 | tf_op jit(solution)/shard_map/ppermute | solution.py:260

commit v5 on v4

--- a/solution.py
+++ b/solution.py
@@ -63,9 +63,12 @@
     inside = (cell >= 0) & (cell < lax.axis_size("gz") * y_tile) & (row < y_tile + 2)
     source = column % ky_groups
     source = jnp.where(source < ky_groups // 2, ky_groups // 2 - 1 - source, source)
-    wave = source * wave_local + column // ky_groups - wave_count // 2
+    half = wave_count // 2
+    row_local = column % half // ky_groups * 2 + column // half
+    wave = source * wave_local + row_local - half
     cos, sin = cos_sin((2 * cell + 1) * wave, int(2 * band_factor * wave_count))
-    return jnp.concatenate([jnp.where(inside, cos, 0.0), jnp.where(inside, -sin, 0.0)], axis=1)
+    cos, sin = jnp.where(inside, cos, 0.0), jnp.where(inside, -sin, 0.0)
+    return [jnp.concatenate([cos[:, at : at + half], sin[:, at : at + half]], axis=1) for at in (0, half)]
 
 
 def dot_nt(a, b):
@@ -73,9 +76,13 @@
 
 
 def x_kernel(ky_groups, level_count, wave_count, amplitudes, out, modes, sem):
-    copy = pltpu.make_async_copy(amplitudes, modes, sem)
-    copy.start()
     wave_local, kx_count = amplitudes.shape[1:]
+    copies = []
+    for part in range(2):
+        for column in range(0, kx_count, kx_count // 2):
+            which = (part, slice(None), pl.ds(column, kx_count // 2))
+            copies.append(pltpu.make_async_copy(amplitudes.at[which], modes.at[which], sem.at[len(copies)]))
+            copies[-1].start()
     per_row = 3 * level_count
     me = lax.axis_index("ky")
     rows = (me * wave_local + lax.broadcasted_iota(jnp.int32, (wave_local, kx_count), 0)).astype(f32)
@@ -91,7 +98,8 @@
     decays = [jnp.exp(jnp.broadcast_to(magnitude[n : n + 1], shape) * depths) for n in range(wave_local)]
     table, cos_centre, sin_centre = x_tables(ky_groups, kx_count, ky_groups)
     table_hi, table_lo = split(table)
-    copy.wait()
+    for copy in copies:
+        copy.wait()
     all_re = modes[0] * cos_centre - modes[1] * sin_centre
     all_im = modes[0] * sin_centre + modes[1] * cos_centre
     parts_re, parts_im = [], []
@@ -149,27 +157,34 @@
     cols = [[received[pl.ds(k * width + t, ky_groups, stride=chunk), :] for t in range(width)] for k in range(4)]
     lane = lax.broadcasted_iota(jnp.int32, (ky_groups, lanes), 1)
     blocks = []
-    for b in range(2 * wave_local):
-        first, offset = divmod(b * per_row, lanes)
-        block = None
+    pair = 2 * per_row
+    for b in range(wave_local):
+        first, offset = divmod(b * pair, lanes)
+        sides = []
         for k in range(4):
-            at = k * per_row
+            at = k % 2 * pair
             shift = (at - offset) % lanes
             piece = pltpu.roll(cols[k][first], shift, axis=1) if shift else cols[k][first]
-            if offset + per_row > lanes:
+            if offset + pair > lanes:
                 rest = pltpu.roll(cols[k][first + 1], shift, axis=1) if shift else cols[k][first + 1]
                 piece = jnp.where(lane < at + lanes - offset, piece, rest)
-            block = piece if block is None else jnp.where(lane < at, block, piece)
-        blocks.append(block)
+            sides.append(piece if k % 2 == 0 else jnp.where(lane < at, sides.pop(), piece))
+        blocks.append(jnp.concatenate(sides, axis=1))
     modes_hi, modes_lo = split(jnp.concatenate(blocks, axis=0))
-    table_hi, table_lo = split(y_tables(y_tile, ky_groups, wave_local, height))
+    tables = y_tables(y_tile, ky_groups, wave_local, height)
+    table_hi, table_lo = split(jnp.concatenate(tables, axis=0))
     both = jnp.dot(jnp.concatenate([table_hi, table_lo], axis=0), modes_hi, preferred_element_type=f32)
-    field = both[:height] + both[height:]
+    field = both[: 2 * height] + both[2 * height :]
     field += jnp.dot(table_hi, modes_lo, preferred_element_type=f32)
-    field = jnp.concatenate([field, jnp.zeros((lanes - height, lanes), f32)], axis=0).T
+    even, odd = field[:height], field[height:]
+    sides = [slice(side, side + lanes) for side in (0, lanes)]
+    field = [even[:, side] + pltpu.roll(odd[:, side], lanes - per_row, axis=1) for side in sides]
+    below_it = jnp.zeros((lanes - height, lanes), f32)
+    field = [jnp.concatenate([side, below_it], axis=0).T for side in field]
+    starts = [(k // 2, k % 2 * pair) for k in range(4)]
     inc = [
-        [field[(k * 3 + c) * level_count : (k * 3 + c + 1) * level_count] for c in range(3)]
-        for k in range(4)
+        [field[side][at + c * level_count : at + (c + 1) * level_count] for c in range(3)]
+        for side, at in starts
     ]
     padded[...] = jnp.zeros_like(padded)
     x_even = lax.axis_index("ky") % 2 == 0
@@ -252,7 +267,7 @@
             out_specs=vmem,
             scratch_shapes=[
                 pltpu.VMEM(amplitudes.shape, f32),
-                pltpu.SemaphoreType.DMA,
+                pltpu.SemaphoreType.DMA((4,)),
             ],
             name="x_transform",
         )(amplitudes)

time: 35.7 us -> 35.7 us (level)
  no operation moved by 1% of the time
where the time goes in v5:
time: 35.7 us; the launch traced here: 35.2 us
  starting transfers between devices  29.2 us (82%)
  Pallas kernels  4.15 us (12%)
  waiting for transfers between devices  1.14 us (3%)
  between operations  0.72 us (2%)
    ppermute x4, starting transfers between devices, on_device(): lax.ppermute(comp, axis, swaps(lax.axis_size(axis), first))  14.6 us
    all_to_all x1, starting transfers between devices, on_device(): received = lax.all_to_all(sent, 'ky', 0, 0, axis_index_groups=[order])  14.6 us
    pallas_call x1, Pallas kernels, on_device(): pl.pallas_call(x_call, out_shape=jax.ShapeDtypeStruct((ky_groups * chunk,...  2.48 us
    pallas_call x1, Pallas kernels, on_device(): pl.pallas_call(y_call, out_shape=(result, result), in_specs=[vmem] * 6, o...  1.67 us
    ppermute x4, waiting for transfers between devices, on_device(): lax.ppermute(comp, axis, swaps(lax.axis_size(axis), first))  1.14 us
  transfers between devices with their start and end apart: 5, of which 1 were waited for; matrix products, arithmetic and copies ran while one was open for 0% of the time, Pallas kernels for 0%

profile of v5, /device:TPU:5, one launch (start us, length us, event | category | flops | bytes accessed | tf_op | source)
XLA Modules:
  0.0 35.2 jit_solution(3866015270249646730)
XLA Ops:
  0.6 2.5 %x_transform.1 = f32[768,128]{1,0:T(8,128)} custom-call(f32[2,8,1024]{2,1,0:T(8,128)} %refs_0_.1), custom_call_target="tpu_custom_call" | custom-call | tf_op jit(solution)/shard_map/x_transform/x_transform/pallas_call | solution.py:263
  3.1 0.0 copy-start
  3.1 14.6 %all-to-all-start = ((f32[64,1,1536]{2,1,0:T(1,128)}), f32[64,1,1536]{2,1,0:T(1,128)S(1)}, u32[]{:S(2)}, u32[]{:S(2)}) async-start(f32[64,1,1536]{2,1,0:T(1,128)} %bitcast.13), calls=%async_computation | async-start | bytes 786432 | tf_op jit(solution)/shard_map/all_to_all | solution.py:280
  17.7 0.0 copy-done
  17.7 2.2 %collective-permute-start = (f32[2,24,32]{2,1,0:T(8,128)S(1)}, f32[2,24,32]{2,1,0:T(8,128)S(1)}, u32[]{:S(2)}, u32[]{:S(2)}) collective-permute-start(f32[2,24,32]{2,1,0:T(8,128)S(1)} %bitcast.8), channel_id=1, source_target_pairs={{1,2},{3,4},{5,6},{2,1},{4,3},{6,5},{9,10},{11,12},{13,14},{10,9},... | collective-permute-start | bytes 18440 | tf_op jit(solution)/shard_map/ppermute | solution.py:275
  19.9 6.6 %collective-permute-start.1 = (f32[2,24,32]{2,1,0:T(8,128)S(1)}, f32[2,24,32]{2,1,0:T(8,128)S(1)}, u32[]{:S(2)}, u32[]{:S(2)}) collective-permute-start(f32[2,24,32]{2,1,0:T(8,128)S(1)} %bitcast.9), channel_id=1, source_target_pairs={{0,1},{2,3},{4,5},{6,7},{1,0},{3,2},{5,4},{7,6},{8,9},{10,11},{12,... | collective-permute-start | bytes 18440 | tf_op jit(solution)/shard_map/ppermute | solution.py:275
  26.5 4.0 %collective-permute-start.2 = (f32[2,24,32]{2,1,0:T(8,128)S(1)}, f32[2,24,32]{2,1,0:T(8,128)S(1)}, u32[]{:S(2)}, u32[]{:S(2)}) collective-permute-start(f32[2,24,32]{2,1,0:T(8,128)S(1)} %bitcast.10), channel_id=1, source_target_pairs={{8,16},{24,32},{40,48},{56,64},{72,80},{88,96},{104,112},{120,128}... | collective-permute-start | bytes 18440 | tf_op jit(solution)/shard_map/ppermute | solution.py:275
  30.5 1.9 %collective-permute-start.3 = (f32[2,24,32]{2,1,0:T(8,128)S(1)}, f32[2,24,32]{2,1,0:T(8,128)S(1)}, u32[]{:S(2)}, u32[]{:S(2)}) collective-permute-start(f32[2,24,32]{2,1,0:T(8,128)S(1)} %bitcast.11), channel_id=1, source_target_pairs={{0,8},{16,24},{32,40},{48,56},{64,72},{80,88},{96,104},{112,120},{... | collective-permute-start | bytes 18440 | tf_op jit(solution)/shard_map/ppermute | solution.py:275
  32.4 0.0 collective-permute-done.refs_2_
  32.4 0.0 collective-permute-done.1.refs_3_
  32.4 0.0 collective-permute-done.2.refs_4_
  32.4 1.1 %collective-permute-done.3.refs_5_ = f32[2,24,32]{2,1,0:T(8,128)S(1)} collective-permute-done((f32[2,24,32]{2,1,0:T(8,128)S(1)}, f32[2,24,32]{2,1,0:T(8,128)S(1)}, u32[]{:S(2)}, u32[]{:S(2)}) %collective-permute-start.3) | collective-permute-done | bytes 6176 | tf_op jit(solution)/shard_map/ppermute | solution.py:275
  33.5 0.0 all-to-all-done
  33.6 1.7 %y_transform.1 = (f32[2,3,8,32]{3,2,1,0:T(8,128)}, f32[2,3,8,32]{3,2,1,0:T(8,128)}) custom-call(f32[768,128]{1,0:T(8,128)S(1)} %bitcast.7, f32[2,24,32]{2,1,0:T(8,128)S(1)} %bitcast.12, f32[2,24,32]{2,1,0:T(8,128)S(1)} %collective-permute-done.refs_2_, f32[2,24,32]{2,1,0:T(8,128)S(1)} %collective-permute-done.1.refs_3_, ...), custom_call_target="tpu_custom_call" | custom-call | tf_op jit(solution)/shard_map/y_transform_and_step/y_transform/pallas_call | solution.py:283
Async XLA Ops:
  3.1 14.6 %copy-start = (f32[2,8,3,32]{3,1,2,0:T(8,128)S(1)}, f32[2,8,3,32]{3,1,2,0:T(8,128)}, u32[]{:S(2)}) copy-start(f32[2,8,3,32]{3,1,2,0:T(8,128)} %param.3) | copy-start | bytes 18436
  3.1 30.4 %all-to-all-start = ((f32[64,1,1536]{2,1,0:T(1,128)}), f32[64,1,1536]{2,1,0:T(1,128)S(1)}, u32[]{:S(2)}, u32[]{:S(2)}) async-start(f32[64,1,1536]{2,1,0:T(1,128)} %bitcast.13), calls=%async_computation | async-start | bytes 786432 | tf_op jit(solution)/shard_map/all_to_all | solution.py:280
  17.7 14.7 %collective-permute-start = (f32[2,24,32]{2,1,0:T(8,128)S(1)}, f32[2,24,32]{2,1,0:T(8,128)S(1)}, u32[]{:S(2)}, u32[]{:S(2)}) collective-permute-start(f32[2,24,32]{2,1,0:T(8,128)S(1)} %bitcast.8), channel_id=1, source_target_pairs={{1,2},{3,4},{5,6},{2,1},{4,3},{6,5},{9,10},{11,12},{13,14},{10,9},... | collective-permute-start | bytes 18440 | tf_op jit(solution)/shard_map/ppermute | solution.py:275
  19.9 12.5 %collective-permute-start.1 = (f32[2,24,32]{2,1,0:T(8,128)S(1)}, f32[2,24,32]{2,1,0:T(8,128)S(1)}, u32[]{:S(2)}, u32[]{:S(2)}) collective-permute-start(f32[2,24,32]{2,1,0:T(8,128)S(1)} %bitcast.9), channel_id=1, source_target_pairs={{0,1},{2,3},{4,5},{6,7},{1,0},{3,2},{5,4},{7,6},{8,9},{10,11},{12,... | collective-permute-start | bytes 18440 | tf_op jit(solution)/shard_map/ppermute | solution.py:275
  26.5 5.9 %collective-permute-start.2 = (f32[2,24,32]{2,1,0:T(8,128)S(1)}, f32[2,24,32]{2,1,0:T(8,128)S(1)}, u32[]{:S(2)}, u32[]{:S(2)}) collective-permute-start(f32[2,24,32]{2,1,0:T(8,128)S(1)} %bitcast.10), channel_id=1, source_target_pairs={{8,16},{24,32},{40,48},{56,64},{72,80},{88,96},{104,112},{120,128}... | collective-permute-start | bytes 18440 | tf_op jit(solution)/shard_map/ppermute | solution.py:275
  30.5 3.1 %collective-permute-start.3 = (f32[2,24,32]{2,1,0:T(8,128)S(1)}, f32[2,24,32]{2,1,0:T(8,128)S(1)}, u32[]{:S(2)}, u32[]{:S(2)}) collective-permute-start(f32[2,24,32]{2,1,0:T(8,128)S(1)} %bitcast.11), channel_id=1, source_target_pairs={{0,8},{16,24},{32,40},{48,56},{64,72},{80,88},{96,104},{112,120},{... | collective-permute-start | bytes 18440 | tf_op jit(solution)/shard_map/ppermute | solution.py:275

commit v6 on v5

--- a/solution.py
+++ b/solution.py
@@ -111,8 +111,9 @@
         parts_re += [-kx * im, -ky * im, k * re]
         parts_im += [kx * re, ky * re, k * im]
     modes_hi, modes_lo = split(jnp.concatenate(parts_re + parts_im, axis=0))
-    product = dot_nt(table_hi, modes_hi)
-    product += dot_nt(table_hi, modes_lo) + dot_nt(table_lo, modes_hi)
+    both = dot_nt(jnp.concatenate([table_hi, table_lo], axis=0), modes_hi)
+    product = both[: 2 * ky_groups] + both[2 * ky_groups :]
+    product += dot_nt(table_hi, modes_lo)
     half = product.shape[0] // 2
     by_cos, by_sin = product[:half], product[half:]
     middle = wave_local * per_row

time: 35.7 us -> 35.5 us (level)
  no operation moved by 1% of the time
where the time goes in v6:
time: 35.5 us; the launch traced here: 35 us
  starting transfers between devices  29.2 us (82%)
  Pallas kernels  3.95 us (11%)
  waiting for transfers between devices  1.14 us (3%)
  between operations  0.72 us (2%)
    ppermute x4, starting transfers between devices, on_device(): lax.ppermute(comp, axis, swaps(lax.axis_size(axis), first))  14.6 us
    all_to_all x1, starting transfers between devices, on_device(): received = lax.all_to_all(sent, 'ky', 0, 0, axis_index_groups=[order])  14.6 us
    pallas_call x1, Pallas kernels, on_device(): pl.pallas_call(x_call, out_shape=jax.ShapeDtypeStruct((ky_groups * chunk,...  2.28 us
    pallas_call x1, Pallas kernels, on_device(): pl.pallas_call(y_call, out_shape=(result, result), in_specs=[vmem] * 6, o...  1.67 us
    ppermute x4, waiting for transfers between devices, on_device(): lax.ppermute(comp, axis, swaps(lax.axis_size(axis), first))  1.14 us
  transfers between devices with their start and end apart: 5, of which 1 were waited for; matrix products, arithmetic and copies ran while one was open for 0% of the time, Pallas kernels for 0%

profile of v6, /device:TPU:5, one launch (start us, length us, event | category | flops | bytes accessed | tf_op | source)
XLA Modules:
  0.0 35.0 jit_solution(16260597492630697507)
XLA Ops:
  0.6 2.3 %x_transform.1 = f32[768,128]{1,0:T(8,128)} custom-call(f32[2,8,1024]{2,1,0:T(8,128)} %refs_0_.1), custom_call_target="tpu_custom_call" | custom-call | tf_op jit(solution)/shard_map/x_transform/x_transform/pallas_call | solution.py:264
  2.9 0.0 copy-start
  2.9 14.6 %all-to-all-start = ((f32[64,1,1536]{2,1,0:T(1,128)}), f32[64,1,1536]{2,1,0:T(1,128)S(1)}, u32[]{:S(2)}, u32[]{:S(2)}) async-start(f32[64,1,1536]{2,1,0:T(1,128)} %bitcast.13), calls=%async_computation | async-start | bytes 786432 | tf_op jit(solution)/shard_map/all_to_all | solution.py:281
  17.5 0.0 copy-done
  17.5 2.2 %collective-permute-start = (f32[2,24,32]{2,1,0:T(8,128)S(1)}, f32[2,24,32]{2,1,0:T(8,128)S(1)}, u32[]{:S(2)}, u32[]{:S(2)}) collective-permute-start(f32[2,24,32]{2,1,0:T(8,128)S(1)} %bitcast.8), channel_id=1, source_target_pairs={{1,2},{3,4},{5,6},{2,1},{4,3},{6,5},{9,10},{11,12},{13,14},{10,9},... | collective-permute-start | bytes 18440 | tf_op jit(solution)/shard_map/ppermute | solution.py:276
  19.7 6.6 %collective-permute-start.1 = (f32[2,24,32]{2,1,0:T(8,128)S(1)}, f32[2,24,32]{2,1,0:T(8,128)S(1)}, u32[]{:S(2)}, u32[]{:S(2)}) collective-permute-start(f32[2,24,32]{2,1,0:T(8,128)S(1)} %bitcast.9), channel_id=1, source_target_pairs={{0,1},{2,3},{4,5},{6,7},{1,0},{3,2},{5,4},{7,6},{8,9},{10,11},{12,... | collective-permute-start | bytes 18440 | tf_op jit(solution)/shard_map/ppermute | solution.py:276
  26.3 4.0 %collective-permute-start.2 = (f32[2,24,32]{2,1,0:T(8,128)S(1)}, f32[2,24,32]{2,1,0:T(8,128)S(1)}, u32[]{:S(2)}, u32[]{:S(2)}) collective-permute-start(f32[2,24,32]{2,1,0:T(8,128)S(1)} %bitcast.10), channel_id=1, source_target_pairs={{8,16},{24,32},{40,48},{56,64},{72,80},{88,96},{104,112},{120,128}... | collective-permute-start | bytes 18440 | tf_op jit(solution)/shard_map/ppermute | solution.py:276
  30.3 1.9 %collective-permute-start.3 = (f32[2,24,32]{2,1,0:T(8,128)S(1)}, f32[2,24,32]{2,1,0:T(8,128)S(1)}, u32[]{:S(2)}, u32[]{:S(2)}) collective-permute-start(f32[2,24,32]{2,1,0:T(8,128)S(1)} %bitcast.11), channel_id=1, source_target_pairs={{0,8},{16,24},{32,40},{48,56},{64,72},{80,88},{96,104},{112,120},{... | collective-permute-start | bytes 18440 | tf_op jit(solution)/shard_map/ppermute | solution.py:276
  32.2 0.0 collective-permute-done.refs_2_
  32.2 0.0 collective-permute-done.1.refs_3_
  32.2 0.0 collective-permute-done.2.refs_4_
  32.2 1.1 %collective-permute-done.3.refs_5_ = f32[2,24,32]{2,1,0:T(8,128)S(1)} collective-permute-done((f32[2,24,32]{2,1,0:T(8,128)S(1)}, f32[2,24,32]{2,1,0:T(8,128)S(1)}, u32[]{:S(2)}, u32[]{:S(2)}) %collective-permute-start.3) | collective-permute-done | bytes 6176 | tf_op jit(solution)/shard_map/ppermute | solution.py:276
  33.3 0.0 all-to-all-done
  33.3 1.7 %y_transform.1 = (f32[2,3,8,32]{3,2,1,0:T(8,128)}, f32[2,3,8,32]{3,2,1,0:T(8,128)}) custom-call(f32[768,128]{1,0:T(8,128)S(1)} %bitcast.7, f32[2,24,32]{2,1,0:T(8,128)S(1)} %bitcast.12, f32[2,24,32]{2,1,0:T(8,128)S(1)} %collective-permute-done.refs_2_, f32[2,24,32]{2,1,0:T(8,128)S(1)} %collective-permute-done.1.refs_3_, ...), custom_call_target="tpu_custom_call" | custom-call | tf_op jit(solution)/shard_map/y_transform_and_step/y_transform/pallas_call | solution.py:284
Async XLA Ops:
  2.9 14.6 %copy-start = (f32[2,8,3,32]{3,1,2,0:T(8,128)S(1)}, f32[2,8,3,32]{3,1,2,0:T(8,128)}, u32[]{:S(2)}) copy-start(f32[2,8,3,32]{3,1,2,0:T(8,128)} %param.3) | copy-start | bytes 18436
  2.9 30.4 %all-to-all-start = ((f32[64,1,1536]{2,1,0:T(1,128)}), f32[64,1,1536]{2,1,0:T(1,128)S(1)}, u32[]{:S(2)}, u32[]{:S(2)}) async-start(f32[64,1,1536]{2,1,0:T(1,128)} %bitcast.13), calls=%async_computation | async-start | bytes 786432 | tf_op jit(solution)/shard_map/all_to_all | solution.py:281
  17.5 14.7 %collective-permute-start = (f32[2,24,32]{2,1,0:T(8,128)S(1)}, f32[2,24,32]{2,1,0:T(8,128)S(1)}, u32[]{:S(2)}, u32[]{:S(2)}) collective-permute-start(f32[2,24,32]{2,1,0:T(8,128)S(1)} %bitcast.8), channel_id=1, source_target_pairs={{1,2},{3,4},{5,6},{2,1},{4,3},{6,5},{9,10},{11,12},{13,14},{10,9},... | collective-permute-start | bytes 18440 | tf_op jit(solution)/shard_map/ppermute | solution.py:276
  19.7 12.5 %collective-permute-start.1 = (f32[2,24,32]{2,1,0:T(8,128)S(1)}, f32[2,24,32]{2,1,0:T(8,128)S(1)}, u32[]{:S(2)}, u32[]{:S(2)}) collective-permute-start(f32[2,24,32]{2,1,0:T(8,128)S(1)} %bitcast.9), channel_id=1, source_target_pairs={{0,1},{2,3},{4,5},{6,7},{1,0},{3,2},{5,4},{7,6},{8,9},{10,11},{12,... | collective-permute-start | bytes 18440 | tf_op jit(solution)/shard_map/ppermute | solution.py:276
  26.3 5.9 %collective-permute-start.2 = (f32[2,24,32]{2,1,0:T(8,128)S(1)}, f32[2,24,32]{2,1,0:T(8,128)S(1)}, u32[]{:S(2)}, u32[]{:S(2)}) collective-permute-start(f32[2,24,32]{2,1,0:T(8,128)S(1)} %bitcast.10), channel_id=1, source_target_pairs={{8,16},{24,32},{40,48},{56,64},{72,80},{88,96},{104,112},{120,128}... | collective-permute-start | bytes 18440 | tf_op jit(solution)/shard_map/ppermute | solution.py:276
  30.3 3.1 %collective-permute-start.3 = (f32[2,24,32]{2,1,0:T(8,128)S(1)}, f32[2,24,32]{2,1,0:T(8,128)S(1)}, u32[]{:S(2)}, u32[]{:S(2)}) collective-permute-start(f32[2,24,32]{2,1,0:T(8,128)S(1)} %bitcast.11), channel_id=1, source_target_pairs={{0,8},{16,24},{32,40},{48,56},{64,72},{80,88},{96,104},{112,120},{... | collective-permute-start | bytes 18440 | tf_op jit(solution)/shard_map/ppermute | solution.py:276
